TPU v7x, 32 devices: a whole 2x2x4 slice. The times are simulated.
32 devices in a mesh: parts: 2 (over y), tile: 4 (over z), shot: 4 (over x, core).
Axes of the slice: x: 2, y: 2, z: 4, core: 2. Of those that a mesh axis runs over, the one named last changes fastest.
Arguments:
- velocity: bfloat16 [128, 32, 128], P(('parts', 'tile'), 'shot'), parts along dimension 0, may hold values from 0.14941406 to 0.44921875
- density: bfloat16 [128, 32, 128], P(('parts', 'tile'), 'shot'), parts along dimension 0, may hold values from 1.796875 to 2.59375
- wave_now: bfloat16 [8, 64, 32, 128], P(('parts', 'shot'), 'tile'), parts along dimension 0, may hold values from -6 to 6
- wave_before: bfloat16 [8, 64, 32, 128], P(('parts', 'shot'), 'tile'), parts along dimension 0, may hold values from -6 to 6
- adjoint_end: bfloat16 [8, 64, 32, 128], P(('parts', 'shot'), 'tile'), parts along dimension 0, may hold values from -6 to 6
- adjoint_after: bfloat16 [8, 64, 32, 128], P(('parts', 'shot'), 'tile'), parts along dimension 0, may hold values from -6 to 6
- source_cell: int32 [8], P(('parts', 'shot')), parts along dimension 0, may hold values from 0 to 262143, as said below
- source_wave: float32 [8, 4], P(('parts', 'shot')), parts along dimension 0, may hold values from -8 to 8
- receiver_cell: int32 [8, 256], P(('parts', 'shot')), parts along dimension 0, may hold values from 0 to 262143, as said below
- residual_traces: float32 [8, 4, 256], P(('parts', 'shot')), parts along dimension 0, may hold values from -6 to 6
- aperture: int32 [8, 2], P(('parts', 'shot')), parts along dimension 0, may hold values from -1 to 3, as said below
Outputs:
- gradient: float32 [128, 32, 128], P(('parts', 'tile'), 'shot'), parts along dimension 0
- wave_end: bfloat16 [8, 64, 32, 128], P(('parts', 'shot'), 'tile'), parts along dimension 0
- adjoint_start: bfloat16 [8, 64, 32, 128], P(('parts', 'shot'), 'tile'), parts along dimension 0
There are 2 independent parts, one for each index of `parts`. A program takes and returns all parts, laid end to end along the dimension named above; each array names one. Nothing has to cross between parts.
Inputs may be any that keep to these rules, and one draw needn't show every extreme that they name: `aperture`: row s lists a run of consecutive tile numbers, 1 to 2 of them, followed by -1 entries. `source_cell`: the flat index x * 32 * 128 + y * 128 + z of the shot's source cell, whose x lies in a tile of the shot's aperture. `receiver_cell`: flat indices as for source_cell, each in a tile of the shot's aperture; a cell may repeat.
All inputs are finite; a program needn't handle non-finite values.
Results may differ from a plain program's by a relative error of at most 0.001.
Values may be sent and summed in bfloat16 or wider, within the bound.
No kernel may reach another device: no remote copies, remote signals or barrier semaphores. Data moves between devices by JAX's collectives and lax.ppermute only.
A program may use at most 64 MiB of HBM per device.

v0:
```python
import jax
import jax.numpy as jnp
from jax import lax
from jax.experimental import pallas as pl
from jax.experimental.pallas import tpu as pltpu
from jax.sharding import PartitionSpec as P

FIRST = (672.0, -168.0, 32.0, -3.0)
SECOND = (8064.0, -1008.0, 128.0, -9.0)
CENTRE_Z = -43008.0
CENTRE_Y = -42.0
SCALE = 5040.0
STEPS = 4
PACK_BYTES = 56 * 1024 * 1024
HALO = 4
VMEM_BYTES = 24 * 1024 * 1024


def vmem():
    return pl.BlockSpec(memory_space=pltpu.VMEM)


def smem():
    return pl.BlockSpec(memory_space=pltpu.SMEM)


def two_terms(values):
    high = values.astype(jnp.bfloat16)
    low = (values - high.astype(jnp.float32)).astype(jnp.bfloat16)
    return high, low


def is_active(aperture_ref, tile):
    found = aperture_ref[0, 0] == tile
    for slot in range(1, aperture_ref.shape[1]):
        found = found | (aperture_ref[0, slot] == tile)
    return found & (tile >= 0)


def layout(aperture_ref, cx):
    tiles = lax.axis_size("tile")
    tile = lax.axis_index("tile")
    even = lax.rem(tile, 2) == 0
    left = is_active(aperture_ref, tile - 1) & (tile > 0)
    right = is_active(aperture_ref, tile + 1) & (tile < tiles - 1)
    own = is_active(aperture_ref, tile)
    a_tile = jnp.where(even, tile + 1, tile - 1)
    b_tile = jnp.where(even, tile - 1, tile + 1)
    a_at = jnp.where(even, 2 * cx, 0)
    b_at = jnp.where(even, 0, 2 * cx)
    a_here = (a_tile >= 0) & (a_tile < tiles)
    b_here = (b_tile >= 0) & (b_tile < tiles)
    a_on = jnp.where(even, right, left)
    b_on = jnp.where(even, left, right)
    return tile, own, left, right, (a_at, a_here, a_on), (b_at, b_here, b_on)


def difference_matrix(shape, along, across, block, centre):
    ahead = lax.rem(along, block) - lax.rem(across, block)
    first = jnp.zeros(shape, jnp.float32)
    second = jnp.where(ahead == 0, centre, 0.0)
    for k in range(1, 5):
        first = jnp.where(ahead == k, FIRST[k - 1], jnp.where(ahead == -k, -FIRST[k - 1], first))
        second = jnp.where((ahead == k) | (ahead == -k), SECOND[k - 1], second)
    return first, second


def pack_kernel(*refs):
    velocity_ref, density_ref, now_ref, before_ref, end_ref, after_ref, model_ref, a_ref, b_ref, sems = refs
    cx = velocity_ref.shape[0]
    even = lax.rem(lax.axis_index("tile"), 2) == 0
    reach = (STEPS - 1) * HALO
    moves = [(velocity_ref, model_ref.at[0:cx]), (density_ref, model_ref.at[cx : 2 * cx])]
    for side, out_ref in enumerate((a_ref, b_ref)):
        first = jnp.where(even == (side == 0), cx - reach, 0)
        base = 0
        for whole_ref, part_ref in ((now_ref, before_ref), (end_ref, after_ref)):
            moves.append((whole_ref.at[0], out_ref.at[base : base + cx]))
            moves.append((part_ref.at[0, pl.ds(first, reach)], out_ref.at[base + cx : base + cx + reach]))
            base += cx + reach
    copies = [pltpu.make_async_copy(src, dst, sems.at[number]) for number, (src, dst) in enumerate(moves)]
    for copy in copies:
        copy.start()
    for copy in copies:
        copy.wait()


def setup_kernel(cx, cells_ref, traces_ref, *refs):
    parts, (along_z_ref, along_y_ref, add_ref, joined_ref) = refs[:-4], refs[-4:]
    ny, nz = add_ref.shape[2:]
    size = parts[0].shape[0]
    for number, part in enumerate(parts):
        joined_ref[number * size : (number + 1) * size, :] = part[...]

    shape = along_z_ref.shape
    rows, cols = (lax.broadcasted_iota(jnp.int32, shape, d) for d in range(2))
    first, second = difference_matrix(shape, rows, cols, nz, CENTRE_Z)
    along_z_ref[...] = jnp.where(cols < nz, first, second).astype(jnp.bfloat16)
    shape = along_y_ref.shape
    rows, cols = (lax.broadcasted_iota(jnp.int32, shape, d) for d in range(2))
    first, second = difference_matrix(shape, cols, rows, ny, CENTRE_Y)
    here = lax.rem(rows, shape[1]) // ny == cols // ny
    along_y_ref[...] = jnp.where(here, jnp.where(rows < shape[1], first, second), 0.0).astype(jnp.bfloat16)

    tile = lax.axis_index("tile")
    count = cells_ref.shape[1]
    cells = cells_ref[...]
    reach = (STEPS - 1) * HALO
    at_row = cells // nz - (tile * cx - reach) * ny
    at_z = lax.rem(cells, nz)
    depth = lax.broadcasted_iota(jnp.int32, (nz, count), 0)
    deep = depth == at_z
    tile = lax.axis_index("tile")
    count = cells_ref.shape[1]
    cells = cells_ref[...]
    reach = (STEPS - 1) * HALO
    at_row = cells // nz - (tile * cx - reach) * ny
    at_z = lax.rem(cells, nz)
    depth = lax.broadcasted_iota(jnp.int32, (nz, count), 0)
    deep = depth == at_z
    values = []
    for step in range(STEPS):
        trace = traces_ref[0, pl.ds(STEPS - 1 - step, 1), :]
        high = trace.astype(jnp.bfloat16).astype(jnp.float32)
        values += [jnp.where(deep, high, 0.0), jnp.where(deep, trace - high, 0.0)]
    values = jnp.concatenate(values, axis=0).astype(jnp.bfloat16)
    chunk = 2 * HALO
    row = lax.broadcasted_iota(jnp.int32, (chunk * ny, count), 0)

    def body(c, carry):
        hot = jnp.where(at_row == row + c * (chunk * ny), 1.0, 0.0).astype(jnp.bfloat16)
        found = lax.dot_general(hot, values, (((1,), (1,)), ((), ())), preferred_element_type=jnp.float32)
        for step in range(STEPS):
            both = found[:, 2 * step * nz : (2 * step + 1) * nz] + found[:, (2 * step + 1) * nz : (2 * step + 2) * nz]
            add_ref[step, pl.ds(c * chunk, chunk)] = both.reshape(chunk, ny, nz)
        return carry

    lax.fori_loop(0, (cx + 2 * reach) // chunk, body, 0)


def matrix_differences(buf, i0, layers, along_z, along_y):
    ny, nz = buf.shape[1:]
    both = jnp.concatenate(two_terms(buf[pl.ds(i0, layers)].reshape(layers * ny, nz)), axis=1)
    from_z = jnp.dot(both, along_z, preferred_element_type=jnp.float32)
    size = along_y.shape[1]
    half = along_y.shape[0] // 2
    first_y, second = [], []
    for base in range(0, layers * ny, size):
        from_y = jnp.dot(along_y, both[base : base + size], preferred_element_type=jnp.float32)
        first_y.append(from_y[:size, :nz] + from_y[:size, nz:])
        if half == size:
            second.append(from_y[size:, :nz] + from_y[size:, nz:] + from_z[base : base + size, nz:])
    shape = (layers, ny, nz)
    first_y, first_z = jnp.concatenate(first_y, axis=0), from_z[:, :nz]
    if not second:
        return first_y.reshape(shape), first_z.reshape(shape), None
    return first_y.reshape(shape), first_z.reshape(shape), jnp.concatenate(second, axis=0).reshape(shape)


def layer_differences(buf, i, summed):
    first = None
    for k in range(1, 5):
        plus, minus = buf[i + k], buf[i - k]
        if summed is not None:
            summed = summed + SECOND[k - 1] * (plus + minus)
        term = FIRST[k - 1] * (plus - minus)
        first = term if first is None else first + term
    return first, summed


def on_segments(step, left, right, cx, work):
    work(cx, cx, True)
    reach = (STEPS - 1 - step) * HALO
    if reach:

        def body(number, carry):
            base = jnp.where(left & (number == 0), cx - reach, 2 * cx)
            work(pl.multiple_of(base, HALO), reach, False)
            return carry

        lax.fori_loop(0, left.astype(jnp.int32) + right.astype(jnp.int32), body, 0)


def march(cur, prev, slopes_ref, courant_ref, along_z, along_y, i0, layers, use):
    first_y, first_z, second = matrix_differences(cur, i0, layers, along_z, along_y)
    for j in range(layers):
        i = i0 + j
        first_x, applied = layer_differences(cur, i, second[j])
        applied = applied - slopes_ref[0, i] * first_x - slopes_ref[1, i] * first_y[j] - slopes_ref[2, i] * first_z[j]
        prev[i] = use(i, j, applied, 2.0 * cur[i] - prev[i] + courant_ref[i] * applied)


def fill(buf, at, rows_ref, first_row, layers, keep):
    ny, nz = buf.shape[1:]
    part = rows_ref[pl.ds(first_row, layers * ny), :].astype(jnp.float32)
    if keep is not None:
        part = jnp.where(keep, part, 0.0)
    buf[pl.ds(at, layers)] = part.reshape(layers, ny, nz)


def fill_fields(now, before, own_now, own_before, from_a, from_b, base, side_a, side_b, cx, ny):
    fill(now, cx, own_now, 0, cx, None)
    fill(before, cx, own_before, 0, cx, None)
    reach = (STEPS - 1) * HALO
    for ref, (at, here, on) in ((from_a, side_a), (from_b, side_b)):
        fill(now, at, ref, base, cx, here)
        fill(before, jnp.where(at == 0, cx - reach, at), ref, base + cx * ny, reach, on)


def clear_sides(buf, left, right, cx):
    zero = jnp.zeros((HALO,) + buf.shape[1:], jnp.float32)

    @pl.when(jnp.logical_not(left))
    def _():
        buf[cx - HALO : cx] = zero

    @pl.when(jnp.logical_not(right))
    def _():
        buf[2 * cx : 2 * cx + HALO] = zero


def model_kernel(cx, ny, nz, shots, blocks, aperture_ref, *refs):
    model_refs = refs[: len(blocks)]
    along_z_ref, along_y_ref, slopes_ref, courant_ref, gain_ref, log_buf = refs[len(blocks) :]
    tile, own, left, right, side_a, side_b = layout(aperture_ref, cx)
    shot = lax.axis_index("shot")
    sides = ((cx, None), (side_a[0], side_a[1]), (side_b[0], side_b[1]))
    block_rows = ny // shots
    size = cx * block_rows

    @pl.when(own)
    def _():
        for ref, held in zip(model_refs, blocks):
            for number, (mask, place) in enumerate(held):
                y0 = pl.multiple_of((shot ^ mask) * block_rows, block_rows)
                at, here = sides[place]
                base = number * 2 * size
                speed = ref[pl.ds(base, size), :].astype(jnp.float32)
                courant = (speed * speed) * (1.0 / SCALE)
                courant_ref[pl.ds(at, cx), pl.ds(y0, block_rows), :] = courant.reshape(cx, block_rows, nz)
                if here is None:
                    gain = speed * (2.0 / SCALE)
                    gain_ref[:, pl.ds(y0, block_rows), :] = gain.reshape(cx, block_rows, nz)
                logs = jnp.log(ref[pl.ds(base + size, size), :].astype(jnp.float32))
                if here is not None:
                    logs = jnp.where(here, logs, 0.0)
                log_buf[pl.ds(at, cx), pl.ds(y0, block_rows), :] = logs.reshape(cx, block_rows, nz)
        along_z, along_y = along_z_ref[...], along_y_ref[...]

        def slopes(i0, layers, inner):
            first_y, first_z, _ = matrix_differences(log_buf, i0, layers, along_z, along_y)
            for j in range(layers):
                slopes_ref[0, i0 + j] = layer_differences(log_buf, i0 + j, None)[0] * (1.0 / 140.0)
                slopes_ref[1, i0 + j] = first_y[j] * (1.0 / 140.0)
                slopes_ref[2, i0 + j] = first_z[j] * (1.0 / 140.0)

        on_segments(0, left, right, cx, slopes)


def window_kernel(
    cx, ny, nz, order, aperture_ref, source_ref, wavelet_ref, along_z_ref, along_y_ref, slopes_ref, courant_ref, gain_ref, add_ref,
    now_ref, before_ref, end_ref, after_ref, from_a, from_b, sums_ref, wave_ref, adjoint_ref, now, before, end, after, stored, image,
):
    tile, own, left, right, side_a, side_b = layout(aperture_ref, cx)
    shot = lax.axis_index("shot")
    block_rows = ny // len(order)

    @pl.when(jnp.logical_not(own))
    def _():
        wave_ref[...] = jnp.zeros_like(wave_ref)
        adjoint_ref[...] = jnp.zeros_like(adjoint_ref)
        sums_ref[...] = jnp.zeros_like(sums_ref)

    @pl.when(own)
    def _():
        half = from_a.shape[0] // 2
        fill_fields(now, before, now_ref, before_ref, from_a, from_b, 0, side_a, side_b, cx, ny)
        fill_fields(end, after, end_ref, after_ref, from_a, from_b, half, side_a, side_b, cx, ny)
        along_z, along_y = along_z_ref[...], along_y_ref[...]
        cell = source_ref[0]
        layer = cell // (ny * nz) - (tile - 1) * cx
        row = lax.rem(cell // nz, ny)
        depth = lax.rem(cell, nz)
        lanes = lax.broadcasted_iota(jnp.int32, (1, nz), 1)
        bufs = (now, before)
        for step in range(STEPS):
            cur, prev = bufs[step % 2], bufs[(step + 1) % 2]

            def work(i0, layers, inner, cur=cur, prev=prev, step=step):
                def use(i, j, applied, updated):
                    if inner:
                        stored[step, j] = applied
                    return updated

                march(cur, prev, slopes_ref, courant_ref, along_z, along_y, i0, layers, use)

            on_segments(step, left, right, cx, work)
            reach = (STEPS - 1 - step) * HALO
            low = jnp.where(left, cx - reach, cx)
            high = jnp.where(right, 2 * cx + reach, 2 * cx)
            value = wavelet_ref[0, step]

            @pl.when((layer >= low) & (layer < high))
            def _(prev=prev, value=value):
                old = prev[layer, pl.ds(row, 1), :]
                prev[layer, pl.ds(row, 1), :] = old + jnp.where(lanes == depth, value, 0.0)

            if step == 0:
                clear_sides(cur, left, right, cx)
        wave_ref[...] = bufs[STEPS % 2][cx : 2 * cx].reshape(cx * ny, nz)

        bufs = (end, after)
        for step in range(STEPS):
            cur, prev = bufs[step % 2], bufs[(step + 1) % 2]

            def work(i0, layers, inner, cur=cur, prev=prev, step=step):
                def use(i, j, applied, updated):
                    updated = updated + add_ref[step, i - (cx - (STEPS - 1) * HALO)]
                    if inner:
                        term = updated * stored[STEPS - 1 - step, j]
                        image[j] = term if step == 0 else image[j] + term
                    return updated

                march(cur, prev, slopes_ref, courant_ref, along_z, along_y, i0, layers, use)

            on_segments(step, left, right, cx, work)
            if step == 0:
                clear_sides(cur, left, right, cx)
        adjoint_ref[...] = bufs[STEPS % 2][cx : 2 * cx].reshape(cx * ny, nz)
        for place, mask in enumerate(order):
            y0 = pl.multiple_of((shot ^ mask) * block_rows, block_rows)
            gain = gain_ref[:, pl.ds(y0, block_rows), :]
            sums_ref[place] = (gain * image[:, pl.ds(y0, block_rows), :]).reshape(cx * block_rows, nz)


def pairs(axis_sizes, kind):
    tiles, shots = axis_sizes
    found = []
    for tile in range(tiles):
        other = tile ^ 1 if kind == "a" else ((tile + 1) ^ 1) - 1
        for shot in range(shots):
            here = tile * shots + shot
            if 0 <= other < tiles:
                found.append((here, other * shots + shot))
            elif shots % 2 == 0:
                found.append((here, tile * shots + (shot ^ 1)))
    return found


def local(
    velocity, density, wave_now, wave_before, adjoint_end, adjoint_after, source_cell, source_wave, receiver_cell, residual_traces,
    aperture,
):
    cx, _, nz = velocity.shape
    ny = wave_now.shape[2]
    shots = lax.axis_size("shot")
    tiles = lax.axis_size("tile")
    rows = cx * ny
    params = pltpu.CompilerParams(vmem_limit_bytes=VMEM_BYTES)

    def swap(x, kind):
        return lax.ppermute(x, ("tile", "shot"), pairs((tiles, shots), kind))

    def cross(x, mask):
        return lax.ppermute(x, "shot", [(i, i ^ mask) for i in range(shots)])

    fields = [x.reshape(rows, nz) for x in (wave_now, wave_before, adjoint_end, adjoint_after)]
    message = jax.ShapeDtypeStruct((2 * (cx + (STEPS - 1) * HALO), ny, nz), jnp.bfloat16)
    model, to_a, to_b = pl.pallas_call(
        pack_kernel,
        out_shape=(jax.ShapeDtypeStruct((2 * cx,) + velocity.shape[1:], jnp.bfloat16), message, message),
        in_specs=[pl.BlockSpec(memory_space=pltpu.HBM)] * 6,
        out_specs=(pl.BlockSpec(memory_space=pltpu.HBM),) * 3,
        scratch_shapes=[pltpu.SemaphoreType.DMA((10,))],
        compiler_params=pltpu.CompilerParams(vmem_limit_bytes=PACK_BYTES),
        cost_estimate=pl.CostEstimate(flops=0, bytes_accessed=2 * 2**20, transcendentals=0),
        name="pack",
    )(velocity, density, wave_now, wave_before, adjoint_end, adjoint_after)
    model, to_a, to_b = (x.reshape(-1, nz) for x in (model, to_a, to_b))

    model_a, model_b = swap(model, "a"), swap(model, "b")
    high = shots // 2
    near = [([(0, 0)], model), ([(0, 1)], model_a), ([(0, 2)], model_b)]
    late = []
    if high:
        near.append(([(high, 0)], cross(model, high)))
        late.append(([(high, 1), (high, 2)], cross(jnp.concatenate([model_a, model_b], axis=0), high)))
    from_a, from_b = swap(to_a, "a"), swap(to_b, "b")

    along_z, along_y, added, joined = pl.pallas_call(
        lambda *refs: setup_kernel(cx, *refs),
        out_shape=(
            jax.ShapeDtypeStruct((2 * nz, 2 * nz), jnp.bfloat16),
            jax.ShapeDtypeStruct((2 * HALO * ny, HALO * ny), jnp.bfloat16),
            jax.ShapeDtypeStruct((STEPS, cx + 2 * (STEPS - 1) * HALO, ny, nz), jnp.float32),
            jax.ShapeDtypeStruct((len(near) * model.shape[0], nz), jnp.bfloat16),
        ),
        in_specs=[vmem()] * (2 + len(near)),
        out_specs=(vmem(),) * 4,
        compiler_params=params,
        cost_estimate=pl.CostEstimate(flops=2 * 10**9, bytes_accessed=4 * 2**20, transcendentals=0),
        name="receivers",
    )(receiver_cell, residual_traces, *[block for _, block in near])

    near = [([name for names, _ in near for name in names], joined)]
    mask = high // 2
    while mask:
        moved = []
        for group in (near, late):
            names = [(m ^ mask, place) for held, _ in group for m, place in held]
            array = group[0][1] if len(group) == 1 else jnp.concatenate([block for _, block in group], axis=0)
            moved.append((names, cross(array, mask)))
        near, late = near + moved[:1], late + moved[1:]
        mask //= 2
    held = near + late

    field = pltpu.VMEM((3 * cx, ny, nz), jnp.float32)
    blocks = tuple(tuple(names) for names, _ in held)
    slopes, courant, gain = pl.pallas_call(
        lambda *refs: model_kernel(cx, ny, nz, shots, blocks, *refs),
        out_shape=(
            jax.ShapeDtypeStruct((3, 3 * cx, ny, nz), jnp.float32),
            jax.ShapeDtypeStruct((3 * cx, ny, nz), jnp.float32),
            jax.ShapeDtypeStruct((cx, ny, nz), jnp.float32),
        ),
        in_specs=[smem()] + [vmem()] * (len(held) + 2),
        out_specs=(vmem(),) * 3,
        scratch_shapes=[field],
        compiler_params=params,
        cost_estimate=pl.CostEstimate(flops=10**6, bytes_accessed=2**20, transcendentals=0),
        name="model",
    )(aperture, *[block for _, block in held], along_z, along_y)

    bits = []
    mask = 1
    while mask < shots:
        bits.append(mask)
        mask *= 2
    order = [0]
    for bit in reversed(bits):
        order = order + [m | bit for m in order]
    order = tuple(order)
    sums, wave_end, adjoint_start = pl.pallas_call(
        lambda *refs: window_kernel(cx, ny, nz, order, *refs),
        out_shape=(
            jax.ShapeDtypeStruct((shots, cx * (ny // shots), nz), jnp.float32),
            jax.ShapeDtypeStruct((rows, nz), jnp.float32),
            jax.ShapeDtypeStruct((rows, nz), jnp.float32),
        ),
        in_specs=[smem()] * 3 + [vmem()] * 12,
        out_specs=(vmem(),) * 3,
        scratch_shapes=[field] * 4 + [pltpu.VMEM((STEPS, cx, ny, nz), jnp.float32), pltpu.VMEM((cx, ny, nz), jnp.float32)],
        compiler_params=params,
        cost_estimate=pl.CostEstimate(flops=10**10, bytes_accessed=16 * 2**20, transcendentals=0),
        name="window",
    )(aperture, source_cell, source_wave, along_z, along_y, slopes, courant, gain, added, *fields, from_a, from_b)
    for bit in bits:
        half = sums.shape[0] // 2
        sums = sums[:half] + cross(sums[half:], bit)
    gradient = sums[0].reshape(cx, ny // shots, nz)
    ends = [x.astype(jnp.bfloat16).reshape(wave_now.shape) for x in (wave_end, adjoint_start)]
    return gradient, ends[0], ends[1]


def solution(mesh):
    stored = P(("parts", "tile"), "shot", None)
    field = P(("parts", "shot"), "tile", None, None)
    return jax.shard_map(
        local,
        mesh=mesh,
        in_specs=(
            stored, stored, field, field, field, field, P(("parts", "shot")), P(("parts", "shot"), None),
            P(("parts", "shot"), None), P(("parts", "shot"), None, None), P(("parts", "shot"), None),
        ),
        out_specs=(stored, field, field),
        check_vma=False,
    )
```

profile of v0, /device:TPU:0, one launch (start us, length us, event | category | flops | bytes accessed | tf_op | source)
XLA Modules:
  0.0 62.2 jit_solution(1245209281538945878)
XLA Ops:
  0.6 31.0 %pack.1 = (bf16[32,8,128]{2,1,0:T(8,128)(2,1)}, bf16[56,32,128]{2,1,0:T(8,128)(2,1)}, bf16[56,32,128]{2,1,0:T(8,128)(2,1)}) custom-call(bf16[16,8,128]{2,1,0:T(8,128)(2,1)} %refs_0_.4, bf16[16,8,128]{2,1,0:T(8,128)(2,1)} %refs_1_.3, bf16[1,16,32,128]{3,2,1,0:T(8,128)(2,1)} %refs_2_.2, bf16[1,16,32,128]{3,2,1,0:T(8,128)(2,1)} %refs_3_.1, ...), custom_call_target="tpu_custom_call" | custom-call | bytes 2097152 | tf_op jit(solution)/shard_map/pack/pallas_call | solution.py:369
  31.6 0.5 collective-permute-start.1
  32.1 4.1 %collective-permute-start = (bf16[256,128]{1,0:T(8,128)(2,1)}, bf16[256,128]{1,0:T(8,128)(2,1)S(1)}, u32[]{:S(2)}, u32[]{:S(2)}) collective-permute-start(bf16[256,128]{1,0:T(8,128)(2,1)} %bitcast.16), channel_id=1, source_target_pairs={{0,4},{1,5},{2,6},{3,7},{4,0},{5,1},{6,2},{7,3},{8,12},{9,13},{10,... | collective-permute-start | bytes 196616 | tf_op jit(solution)/shard_map/ppermute | solution.py:362
  36.3 1.5 %collective-permute-start.2 = (bf16[256,128]{1,0:T(8,128)(2,1)}, bf16[256,128]{1,0:T(8,128)(2,1)S(1)}, u32[]{:S(2)}, u32[]{:S(2)}) collective-permute-start(bf16[256,128]{1,0:T(8,128)(2,1)} %bitcast.17), channel_id=1, source_target_pairs={{0,2},{1,3},{2,0},{3,1},{4,6},{5,7},{6,4},{7,5},{8,10},{9,11},{10,... | collective-permute-start | bytes 196616 | tf_op jit(solution)/shard_map/ppermute | solution.py:365
  37.8 1.3 %collective-permute-done.refs_3_ = bf16[256,128]{1,0:T(8,128)(2,1)S(1)} collective-permute-done((bf16[256,128]{1,0:T(8,128)(2,1)}, bf16[256,128]{1,0:T(8,128)(2,1)S(1)}, u32[]{:S(2)}, u32[]{:S(2)}) %collective-permute-start) | collective-permute-done | bytes 65568 | tf_op jit(solution)/shard_map/ppermute | solution.py:362
  39.1 0.0 copy-start
  39.1 1.6 %collective-permute-start.4 = (bf16[512,128]{1,0:T(8,128)(2,1)S(1)}, bf16[512,128]{1,0:T(8,128)(2,1)S(1)}, u32[]{:S(2)}, u32[]{:S(2)}) collective-permute-start(bf16[512,128]{1,0:T(8,128)(2,1)S(1)} %pad_maximum_fusion), channel_id=1, source_target_pairs={{0,2},{1,3},{2,0},{3,1},{4,6},{5,7},{6,4},{7,5},{8,10},{9,11},{10,... | collective-permute-start | bytes 393224 | tf_op jit(solution)/shard_map/ppermute | solution.py:365
  40.8 0.8 %copy-done.5 = bf16[32,8,128]{2,1,0:T(8,128)(2,1)S(1)} copy-done((bf16[32,8,128]{2,1,0:T(8,128)(2,1)S(1)}, bf16[32,8,128]{2,1,0:T(8,128)(2,1)}, u32[]{:S(2)}) %copy-start.5) | copy-done | bytes 65560
  41.6 0.7 %copy-done.6 = f32[1,4,256]{2,1,0:T(4,128)S(1)} copy-done((f32[1,4,256]{2,1,0:T(4,128)S(1)}, f32[1,4,256]{2,1,0:T(4,128)}, u32[]{:S(2)}) %copy-start.6) | copy-done | bytes 4120
  42.3 0.7 %copy-done.7 = s32[1,256]{1,0:T(1,128)S(1)} copy-done((s32[1,256]{1,0:T(1,128)S(1)}, s32[1,256]{1,0:T(1,128)}, u32[]{:S(2)}) %copy-start.7) | copy-done | bytes 1048
  43.0 2.0 %receivers.1 = (bf16[256,256]{1,0:T(8,128)(2,1)S(1)}, bf16[256,128]{1,0:T(8,128)(2,1)S(1)}, f32[4,40,32,128]{3,2,1,0:T(8,128)S(1)}, bf16[1024,128]{1,0:T(8,128)(2,1)S(1)}) custom-call(s32[1,256]{1,0:T(1,128)S(1)} %copy-done.7, f32[1,4,256]{2,1,0:T(4,128)S(1)} %copy-done.6, bf16[256,128]{1,0:T(8,128)(2,1)S(1)} %bitcast.18, ...), custom_call_target="tpu_custom_call" | custom-call | flops 2000000000 | bytes 4194304 | tf_op jit(solution)/shard_map/receivers/pallas_call | solution.py:390
  44.9 0.1 collective-permute-start.3
  45.0 0.5 collective-permute-start.5
  46.2 0.6 collective-permute-done.5.refs_4_
  46.7 1.3 %model.1 = (f32[3,48,32,128]{3,2,1,0:T(8,128)S(1)}, f32[48,32,128]{2,1,0:T(8,128)S(1)}, f32[16,32,128]{2,1,0:T(8,128)S(1)}) custom-call(s32[1,2]{1,0:T(1,128)S(1)} %copy-done.4, bf16[1024,128]{1,0:T(8,128)(2,1)S(1)} %get-tuple-element.19.refs_1_, bf16[1024,128]{1,0:T(8,128)(2,1)S(1)} %collective-permute-done.3.refs_2_, ...), custom_call_target="tpu_custom_call" | custom-call | flops 1000000 | bytes 1048576 | tf_op jit(solution)/shard_map/model/pallas_call | solution.py:419
  48.0 1.4 %collective-permute-done.6.refs_13_ = bf16[1792,128]{1,0:T(8,128)(2,1)S(1)} collective-permute-done((bf16[1792,128]{1,0:T(8,128)(2,1)}, bf16[1792,128]{1,0:T(8,128)(2,1)S(1)}, u32[]{:S(2)}, u32[]{:S(2)}) %collective-permute-start.6) | collective-permute-done | bytes 458784 | tf_op jit(solution)/shard_map/ppermute | solution.py:362
  49.4 5.2 %window.1 = (f32[4,128,128]{2,1,0:T(8,128)S(1)}, f32[512,128]{1,0:T(8,128)S(1)}, f32[512,128]{1,0:T(8,128)S(1)}) custom-call(s32[1,2]{1,0:T(1,128)S(1)} %copy-done.4, s32[1]{0:T(128)S(6)} %copy.14.refs_1_, f32[1,4]{1,0:T(1,128)S(1)} %copy-done.8, bf16[256,256]{1,0:T(8,128)(2,1)S(1)} %get-tuple-element.17.refs_5_.refs_3_, ...), custom_call_target="tpu_custom_call" | custom-call | flops 10000000000 | bytes 16777216 | tf_op jit(solution)/shard_map/window/pallas_call | solution.py:443
  54.7 0.1 collective-permute-start.8
  54.8 1.3 %collective-permute-done.8 = f32[2,128,128]{2,1,0:T(8,128)S(1)} collective-permute-done((f32[2,128,128]{2,1,0:T(8,128)S(1)}, f32[2,128,128]{2,1,0:T(8,128)S(1)}, u32[]{:S(2)}, u32[]{:S(2)}) %collective-permute-start.8) | collective-permute-done | bytes 131104 | tf_op jit(solution)/shard_map/ppermute | solution.py:365
  56.1 2.8 %collective-permute-start.9 = (f32[1,128,128]{2,1,0:T(8,128)S(1)}, f32[1,128,128]{2,1,0:T(8,128)S(1)}, u32[]{:S(2)}, u32[]{:S(2)}) collective-permute-start(f32[1,128,128]{2,1,0:T(8,128)S(1)} %slice.17), channel_id=1, source_target_pairs={{0,2},{1,3},{2,0},{3,1},{4,6},{5,7},{6,4},{7,5},{8,10},{9,11},{10,... | collective-permute-start | bytes 196616 | tf_op jit(solution)/shard_map/ppermute | solution.py:365
  58.9 0.7 %convert_element_type.6 = bf16[512,128]{1,0:T(8,128)(2,1)} convert(f32[512,128]{1,0:T(8,128)S(1)} %get-tuple-element.27) | non-fusion elementwise | flops 65536 | bytes 393216 | tf_op jit(solution)/shard_map/convert_element_type | solution.py:461
  59.6 0.7 %convert_element_type.7 = bf16[512,128]{1,0:T(8,128)(2,1)} convert(f32[512,128]{1,0:T(8,128)S(1)} %get-tuple-element.28) | non-fusion elementwise | flops 65536 | bytes 393216 | tf_op jit(solution)/shard_map/convert_element_type | solution.py:461
  60.3 1.3 %collective-permute-done.9 = f32[1,128,128]{2,1,0:T(8,128)S(1)} collective-permute-done((f32[1,128,128]{2,1,0:T(8,128)S(1)}, f32[1,128,128]{2,1,0:T(8,128)S(1)}, u32[]{:S(2)}, u32[]{:S(2)}) %collective-permute-start.9) | collective-permute-done | bytes 65568 | tf_op jit(solution)/shard_map/ppermute | solution.py:365
  61.5 0.6 %fusion = f32[16,8,128]{2,1,0:T(8,128)} fusion(f32[1,128,128]{2,1,0:T(8,128)S(1)} %collective-permute-done.9, f32[2,128,128]{2,1,0:T(8,128)S(1)} %slice_add_fusion), kind=kLoop, calls=%fused_computation.3 | loop fusion | flops 16384 | bytes 196608 | tf_op jit(solution)/shard_map/reshape;squeeze | solution.py:460
  (25 shorter events, 0.1 us)
Async XLA Ops:
  31.6 6.2 %collective-permute-start.1 = (bf16[256,128]{1,0:T(8,128)(2,1)}, bf16[256,128]{1,0:T(8,128)(2,1)S(1)}, u32[]{:S(2)}, u32[]{:S(2)}) collective-permute-start(bf16[256,128]{1,0:T(8,128)(2,1)} %bitcast.15), channel_id=1, source_target_pairs={{0,1},{1,0},{2,3},{3,2},{4,8},{5,9},{6,10},{7,11},{8,4},{9,5},{10,... | collective-permute-start | bytes 196616 | tf_op jit(solution)/shard_map/ppermute | solution.py:362
  32.1 6.9 %collective-permute-start = (bf16[256,128]{1,0:T(8,128)(2,1)}, bf16[256,128]{1,0:T(8,128)(2,1)S(1)}, u32[]{:S(2)}, u32[]{:S(2)}) collective-permute-start(bf16[256,128]{1,0:T(8,128)(2,1)} %bitcast.16), channel_id=1, source_target_pairs={{0,4},{1,5},{2,6},{3,7},{4,0},{5,1},{6,2},{7,3},{8,12},{9,13},{10,... | collective-permute-start | bytes 196616 | tf_op jit(solution)/shard_map/ppermute | solution.py:362
  36.3 4.5 %collective-permute-start.2 = (bf16[256,128]{1,0:T(8,128)(2,1)}, bf16[256,128]{1,0:T(8,128)(2,1)S(1)}, u32[]{:S(2)}, u32[]{:S(2)}) collective-permute-start(bf16[256,128]{1,0:T(8,128)(2,1)} %bitcast.17), channel_id=1, source_target_pairs={{0,2},{1,3},{2,0},{3,1},{4,6},{5,7},{6,4},{7,5},{8,10},{9,11},{10,... | collective-permute-start | bytes 196616 | tf_op jit(solution)/shard_map/ppermute | solution.py:365
  37.8 11.6 %collective-permute-start.6 = (bf16[1792,128]{1,0:T(8,128)(2,1)}, bf16[1792,128]{1,0:T(8,128)(2,1)S(1)}, u32[]{:S(2)}, u32[]{:S(2)}) collective-permute-start(bf16[1792,128]{1,0:T(8,128)(2,1)} %bitcast.22), channel_id=1, source_target_pairs={{0,4},{1,5},{2,6},{3,7},{4,0},{5,1},{6,2},{7,3},{8,12},{9,13},{10,... | collective-permute-start | bytes 1376264 | tf_op jit(solution)/shard_map/ppermute | solution.py:362
  37.8 11.6 %collective-permute-start.7 = (bf16[1792,128]{1,0:T(8,128)(2,1)}, bf16[1792,128]{1,0:T(8,128)(2,1)S(1)}, u32[]{:S(2)}, u32[]{:S(2)}) collective-permute-start(bf16[1792,128]{1,0:T(8,128)(2,1)} %bitcast.21), channel_id=1, source_target_pairs={{0,1},{1,0},{2,3},{3,2},{4,8},{5,9},{6,10},{7,11},{8,4},{9,5},{10,... | collective-permute-start | bytes 1376264 | tf_op jit(solution)/shard_map/ppermute | solution.py:362
  39.1 10.3 %copy-start.8 = (f32[1,4]{1,0:T(1,128)S(1)}, f32[1,4]{1,0:T(1,128)}, u32[]{:S(2)}) copy-start(f32[1,4]{1,0:T(1,128)} %refs_2_.3) | copy-start | bytes 52
  39.1 7.6 %copy-start.4 = (s32[1,2]{1,0:T(1,128)S(1)}, s32[1,2]{1,0:T(1,128)}, u32[]{:S(2)}) copy-start(s32[1,2]{1,0:T(1,128)} %refs_0_.7) | copy-start | bytes 28
  39.1 10.3 %copy-start = (bf16[1,16,32,128]{3,2,1,0:T(8,128)(2,1)S(1)}, bf16[1,16,32,128]{3,2,1,0:T(8,128)(2,1)}, u32[]{:S(2)}) copy-start(bf16[1,16,32,128]{3,2,1,0:T(8,128)(2,1)} %refs_2_.2) | copy-start | bytes 393220
  39.1 10.3 %copy-start.1 = (bf16[1,16,32,128]{3,2,1,0:T(8,128)(2,1)S(1)}, bf16[1,16,32,128]{3,2,1,0:T(8,128)(2,1)}, u32[]{:S(2)}) copy-start(bf16[1,16,32,128]{3,2,1,0:T(8,128)(2,1)} %refs_3_.1) | copy-start | bytes 393220
  39.1 10.3 %copy-start.2 = (bf16[1,16,32,128]{3,2,1,0:T(8,128)(2,1)S(1)}, bf16[1,16,32,128]{3,2,1,0:T(8,128)(2,1)}, u32[]{:S(2)}) copy-start(bf16[1,16,32,128]{3,2,1,0:T(8,128)(2,1)} %refs_4_.1) | copy-start | bytes 393220
  39.1 10.3 %copy-start.3 = (bf16[1,16,32,128]{3,2,1,0:T(8,128)(2,1)S(1)}, bf16[1,16,32,128]{3,2,1,0:T(8,128)(2,1)}, u32[]{:S(2)}) copy-start(bf16[1,16,32,128]{3,2,1,0:T(8,128)(2,1)} %refs_5_.1) | copy-start | bytes 393220
  39.1 5.9 %collective-permute-start.4 = (bf16[512,128]{1,0:T(8,128)(2,1)S(1)}, bf16[512,128]{1,0:T(8,128)(2,1)S(1)}, u32[]{:S(2)}, u32[]{:S(2)}) collective-permute-start(bf16[512,128]{1,0:T(8,128)(2,1)S(1)} %pad_maximum_fusion), channel_id=1, source_target_pairs={{0,2},{1,3},{2,0},{3,1},{4,6},{5,7},{6,4},{7,5},{8,10},{9,11},{10,... | collective-permute-start | bytes 393224 | tf_op jit(solution)/shard_map/ppermute | solution.py:365
  40.8 0.8 %copy-start.5 = (bf16[32,8,128]{2,1,0:T(8,128)(2,1)S(1)}, bf16[32,8,128]{2,1,0:T(8,128)(2,1)}, u32[]{:S(2)}) copy-start(bf16[32,8,128]{2,1,0:T(8,128)(2,1)} %get-tuple-element.16) | copy-start | bytes 196612
  41.6 0.7 %copy-start.6 = (f32[1,4,256]{2,1,0:T(4,128)S(1)}, f32[1,4,256]{2,1,0:T(4,128)}, u32[]{:S(2)}) copy-start(f32[1,4,256]{2,1,0:T(4,128)} %refs_1_.4) | copy-start | bytes 12292
  42.3 0.7 %copy-start.7 = (s32[1,256]{1,0:T(1,128)S(1)}, s32[1,256]{1,0:T(1,128)}, u32[]{:S(2)}) copy-start(s32[1,256]{1,0:T(1,128)} %refs_0_.5) | copy-start | bytes 3076
  44.9 1.8 %collective-permute-start.3 = (bf16[1024,128]{1,0:T(8,128)(2,1)S(1)}, bf16[1024,128]{1,0:T(8,128)(2,1)S(1)}, u32[]{:S(2)}, u32[]{:S(2)}) collective-permute-start(bf16[1024,128]{1,0:T(8,128)(2,1)S(1)} %get-tuple-element.19.refs_1_), channel_id=1, source_target_pairs={{0,1},{1,0},{2,3},{3,2},{4,5},{5,4},{6,7},{7,6},{8,9},{9,8},{10,11... | collective-permute-start | bytes 786440 | tf_op jit(solution)/shard_map/ppermute | solution.py:365
  45.0 1.7 %collective-permute-start.5 = (bf16[512,128]{1,0:T(8,128)(2,1)S(1)}, bf16[512,128]{1,0:T(8,128)(2,1)S(1)}, u32[]{:S(2)}, u32[]{:S(2)}) collective-permute-start(bf16[512,128]{1,0:T(8,128)(2,1)S(1)} %collective-permute-done.4.refs_3_), channel_id=1, source_target_pairs={{0,1},{1,0},{2,3},{3,2},{4,5},{5,4},{6,7},{7,6},{8,9},{9,8},{10,11... | collective-permute-start | bytes 393224 | tf_op jit(solution)/shard_map/ppermute | solution.py:365
  54.7 1.4 %collective-permute-start.8 = (f32[2,128,128]{2,1,0:T(8,128)S(1)}, f32[2,128,128]{2,1,0:T(8,128)S(1)}, u32[]{:S(2)}, u32[]{:S(2)}) collective-permute-start(f32[2,128,128]{2,1,0:T(8,128)S(1)} %slice.13), channel_id=1, source_target_pairs={{0,1},{1,0},{2,3},{3,2},{4,5},{5,4},{6,7},{7,6},{8,9},{9,8},{10,11... | collective-permute-start | bytes 393224 | tf_op jit(solution)/shard_map/ppermute | solution.py:365
  56.1 5.4 %collective-permute-start.9 = (f32[1,128,128]{2,1,0:T(8,128)S(1)}, f32[1,128,128]{2,1,0:T(8,128)S(1)}, u32[]{:S(2)}, u32[]{:S(2)}) collective-permute-start(f32[1,128,128]{2,1,0:T(8,128)S(1)} %slice.17), channel_id=1, source_target_pairs={{0,2},{1,3},{2,0},{3,1},{4,6},{5,7},{6,4},{7,5},{8,10},{9,11},{10,... | collective-permute-start | bytes 196616 | tf_op jit(solution)/shard_map/ppermute | solution.py:365
where the time goes:
time: 62.8 us; the launch traced here: 62.2 us
  Pallas kernels  39.4 us (63%)
  starting transfers between devices  11.2 us (18%)
  waiting for transfers between devices  5.88 us (9%)
  local copies, waits for them, and re-layouts  2.26 us (4%)
  other arithmetic  2 us (3%)
  between operations  1.44 us (2%)
    pallas_call x1, Pallas kernels, local(): pl.pallas_call(pack_kernel, out_shape=(jax.ShapeDtypeStruct((2 * cx,) + v...  31 us
    ppermute x6, starting transfers between devices, cross(): return lax.ppermute(x, 'shot', [(i, i ^ mask) for i in range(shots)])  6.51 us
    pallas_call x1, Pallas kernels, local(): pl.pallas_call(lambda *refs: window_kernel(cx, ny, nz, order, *refs), out...  5.23 us
    ppermute x4, starting transfers between devices, swap(): return lax.ppermute(x, ('tile', 'shot'), pairs((tiles, shots), kind))  4.67 us
    ppermute x6, waiting for transfers between devices, cross(): return lax.ppermute(x, 'shot', [(i, i ^ mask) for i in range(shots)])  3.17 us
    ppermute x4, waiting for transfers between devices, swap(): return lax.ppermute(x, ('tile', 'shot'), pairs((tiles, shots), kind))  2.71 us
    unnamed x18, local copies, waits for them, and re-layouts  2.24 us
    pallas_call x1, Pallas kernels, local(): pl.pallas_call(lambda *refs: setup_kernel(cx, *refs), out_shape=(jax.Shap...  1.95 us
  transfers between devices with their start and end apart: 10, of which 5 were waited for; matrix products, arithmetic and copies ran while one was open for 2% of the time, Pallas kernels for 5%

commit v1 on v0

--- a/solution.py
+++ b/solution.py
@@ -181,13 +181,19 @@
         lax.fori_loop(0, left.astype(jnp.int32) + right.astype(jnp.int32), body, 0)
 
 
-def march(cur, prev, slopes_ref, courant_ref, along_z, along_y, i0, layers, use):
-    first_y, first_z, second = matrix_differences(cur, i0, layers, along_z, along_y)
+def march(pairs, slopes_ref, courant_ref, along_z, along_y, i0, layers, use):
+    parts = [matrix_differences(cur, i0, layers, along_z, along_y) for cur, _ in pairs]
     for j in range(layers):
         i = i0 + j
-        first_x, applied = layer_differences(cur, i, second[j])
-        applied = applied - slopes_ref[0, i] * first_x - slopes_ref[1, i] * first_y[j] - slopes_ref[2, i] * first_z[j]
-        prev[i] = use(i, j, applied, 2.0 * cur[i] - prev[i] + courant_ref[i] * applied)
+        slopes = [slopes_ref[axis, i] for axis in range(3)]
+        courant = courant_ref[i]
+        steps = []
+        for (cur, prev), (first_y, first_z, second) in zip(pairs, parts):
+            first_x, applied = layer_differences(cur, i, second[j])
+            applied = applied - slopes[0] * first_x - slopes[1] * first_y[j] - slopes[2] * first_z[j]
+            steps.append((applied, 2.0 * cur[i] - prev[i] + courant * applied))
+        for (_, prev), updated in zip(pairs, use(i, j, steps)):
+            prev[i] = updated
 
 
 def fill(buf, at, rows_ref, first_row, layers, keep):
@@ -259,7 +265,8 @@
 
 def window_kernel(
     cx, ny, nz, order, aperture_ref, source_ref, wavelet_ref, along_z_ref, along_y_ref, slopes_ref, courant_ref, gain_ref, add_ref,
-    now_ref, before_ref, end_ref, after_ref, from_a, from_b, sums_ref, wave_ref, adjoint_ref, now, before, end, after, stored, image,
+    now_ref, before_ref, end_ref, after_ref, from_a, from_b, sums_ref, wave_ref, adjoint_ref, now, before, end, after, applied_held,
+    adjoint_held, image,
 ):
     tile, own, left, right, side_a, side_b = layout(aperture_ref, cx)
     shot = lax.axis_index("shot")
@@ -282,51 +289,42 @@
         row = lax.rem(cell // nz, ny)
         depth = lax.rem(cell, nz)
         lanes = lax.broadcasted_iota(jnp.int32, (1, nz), 1)
-        bufs = (now, before)
+        forward, adjoint = (now, before), (end, after)
         for step in range(STEPS):
-            cur, prev = bufs[step % 2], bufs[(step + 1) % 2]
-
-            def work(i0, layers, inner, cur=cur, prev=prev, step=step):
-                def use(i, j, applied, updated):
-                    if inner:
-                        stored[step, j] = applied
-                    return updated
-
-                march(cur, prev, slopes_ref, courant_ref, along_z, along_y, i0, layers, use)
+            here = tuple((bufs[step % 2], bufs[(step + 1) % 2]) for bufs in (forward, adjoint))
+
+            def work(i0, layers, inner, here=here, step=step):
+                def use(i, j, steps):
+                    (applied, wave), (_, back) = steps
+                    back = back + add_ref[step, i - (cx - (STEPS - 1) * HALO)]
+                    if inner and 2 * step < STEPS:
+                        applied_held[step, j] = applied
+                        adjoint_held[step, j] = back
+                    elif inner:
+                        other = STEPS - 1 - step
+                        terms = applied * adjoint_held[other, j] + back * applied_held[other, j]
+                        image[j] = terms if 2 * step == STEPS else image[j] + terms
+                    return wave, back
+
+                march(here, slopes_ref, courant_ref, along_z, along_y, i0, layers, use)
 
             on_segments(step, left, right, cx, work)
             reach = (STEPS - 1 - step) * HALO
             low = jnp.where(left, cx - reach, cx)
             high = jnp.where(right, 2 * cx + reach, 2 * cx)
             value = wavelet_ref[0, step]
+            made = here[0][1]
 
             @pl.when((layer >= low) & (layer < high))
-            def _(prev=prev, value=value):
-                old = prev[layer, pl.ds(row, 1), :]
-                prev[layer, pl.ds(row, 1), :] = old + jnp.where(lanes == depth, value, 0.0)
+            def _(made=made, value=value):
+                old = made[layer, pl.ds(row, 1), :]
+                made[layer, pl.ds(row, 1), :] = old + jnp.where(lanes == depth, value, 0.0)
 
             if step == 0:
-                clear_sides(cur, left, right, cx)
-        wave_ref[...] = bufs[STEPS % 2][cx : 2 * cx].reshape(cx * ny, nz)
-
-        bufs = (end, after)
-        for step in range(STEPS):
-            cur, prev = bufs[step % 2], bufs[(step + 1) % 2]
-
-            def work(i0, layers, inner, cur=cur, prev=prev, step=step):
-                def use(i, j, applied, updated):
-                    updated = updated + add_ref[step, i - (cx - (STEPS - 1) * HALO)]
-                    if inner:
-                        term = updated * stored[STEPS - 1 - step, j]
-                        image[j] = term if step == 0 else image[j] + term
-                    return updated
-
-                march(cur, prev, slopes_ref, courant_ref, along_z, along_y, i0, layers, use)
-
-            on_segments(step, left, right, cx, work)
-            if step == 0:
-                clear_sides(cur, left, right, cx)
-        adjoint_ref[...] = bufs[STEPS % 2][cx : 2 * cx].reshape(cx * ny, nz)
+                clear_sides(now, left, right, cx)
+                clear_sides(end, left, right, cx)
+        wave_ref[...] = forward[STEPS % 2][cx : 2 * cx].reshape(cx * ny, nz)
+        adjoint_ref[...] = adjoint[STEPS % 2][cx : 2 * cx].reshape(cx * ny, nz)
         for place, mask in enumerate(order):
             y0 = pl.multiple_of((shot ^ mask) * block_rows, block_rows)
             gain = gain_ref[:, pl.ds(y0, block_rows), :]
@@ -370,13 +368,15 @@
         pack_kernel,
         out_shape=(jax.ShapeDtypeStruct((2 * cx,) + velocity.shape[1:], jnp.bfloat16), message, message),
         in_specs=[pl.BlockSpec(memory_space=pltpu.HBM)] * 6,
-        out_specs=(pl.BlockSpec(memory_space=pltpu.HBM),) * 3,
+        out_specs=(vmem(),) * 3,
         scratch_shapes=[pltpu.SemaphoreType.DMA((10,))],
         compiler_params=pltpu.CompilerParams(vmem_limit_bytes=PACK_BYTES),
         cost_estimate=pl.CostEstimate(flops=0, bytes_accessed=2 * 2**20, transcendentals=0),
         name="pack",
     )(velocity, density, wave_now, wave_before, adjoint_end, adjoint_after)
     model, to_a, to_b = (x.reshape(-1, nz) for x in (model, to_a, to_b))
+
+    from_a, from_b = swap(to_a, "a"), swap(to_b, "b")
 
     model_a, model_b = swap(model, "a"), swap(model, "b")
     high = shots // 2
@@ -385,7 +385,6 @@
     if high:
         near.append(([(high, 0)], cross(model, high)))
         late.append(([(high, 1), (high, 2)], cross(jnp.concatenate([model_a, model_b], axis=0), high)))
-    from_a, from_b = swap(to_a, "a"), swap(to_b, "b")
 
     along_z, along_y, added, joined = pl.pallas_call(
         lambda *refs: setup_kernel(cx, *refs),
@@ -449,7 +448,7 @@
         ),
         in_specs=[smem()] * 3 + [vmem()] * 12,
         out_specs=(vmem(),) * 3,
-        scratch_shapes=[field] * 4 + [pltpu.VMEM((STEPS, cx, ny, nz), jnp.float32), pltpu.VMEM((cx, ny, nz), jnp.float32)],
+        scratch_shapes=[field] * 4 + [pltpu.VMEM((STEPS // 2, cx, ny, nz), jnp.float32)] * 2 + [pltpu.VMEM((cx, ny, nz), jnp.float32)],
         compiler_params=params,
         cost_estimate=pl.CostEstimate(flops=10**10, bytes_accessed=16 * 2**20, transcendentals=0),
         name="window",

time: 62.8 us -> 32.4 us (0.52)
  the two profiles are of different devices: /device:TPU:0 before, /device:TPU:8 now
where the time goes in v1:
time: 32.4 us
  Pallas kernels  12.3 us (38%)
  starting transfers between devices  7.92 us (24%)
  waiting for transfers between devices  6.46 us (20%)
  local copies, waits for them, and re-layouts  2.26 us (7%)
  other arithmetic  2 us (6%)
  between operations  1.45 us (4%)
    pallas_call x1, Pallas kernels, local(): pl.pallas_call(lambda *refs: window_kernel(cx, ny, nz, order, *refs), out...  6.46 us
    ppermute x6, waiting for transfers between devices, cross(): return lax.ppermute(x, 'shot', [(i, i ^ mask) for i in range(shots)])  4.81 us
    ppermute x4, starting transfers between devices, swap(): return lax.ppermute(x, ('tile', 'shot'), pairs((tiles, shots), kind))  4.12 us
    ppermute x6, starting transfers between devices, cross(): return lax.ppermute(x, 'shot', [(i, i ^ mask) for i in range(shots)])  3.8 us
    pallas_call x1, Pallas kernels, local(): pl.pallas_call(pack_kernel, out_shape=(jax.ShapeDtypeStruct((2 * cx,) + v...  2.31 us
    unnamed x18, local copies, waits for them, and re-layouts  2.24 us
    pallas_call x1, Pallas kernels, local(): pl.pallas_call(lambda *refs: setup_kernel(cx, *refs), out_shape=(jax.Shap...  1.95 us
    ppermute x4, waiting for transfers between devices, swap(): return lax.ppermute(x, ('tile', 'shot'), pairs((tiles, shots), kind))  1.65 us
  transfers between devices with their start and end apart: 10, of which 5 were waited for; matrix products, arithmetic and copies ran while one was open for 4% of the time, Pallas kernels for 11%

profile of v1, /device:TPU:8, one launch (start us, length us, event | category | flops | bytes accessed | tf_op | source)
XLA Modules:
  0.0 32.4 jit_solution(11808080109447538398)
XLA Ops:
  0.6 2.3 %pack.1 = (bf16[32,8,128]{2,1,0:T(8,128)(2,1)}, bf16[56,32,128]{2,1,0:T(8,128)(2,1)}, bf16[56,32,128]{2,1,0:T(8,128)(2,1)}) custom-call(bf16[16,8,128]{2,1,0:T(8,128)(2,1)} %refs_0_.4, bf16[16,8,128]{2,1,0:T(8,128)(2,1)} %refs_1_.3, bf16[1,16,32,128]{3,2,1,0:T(8,128)(2,1)} %refs_2_.2, bf16[1,16,32,128]{3,2,1,0:T(8,128)(2,1)} %refs_3_.1, ...), custom_call_target="tpu_custom_call" | custom-call | bytes 2097152 | tf_op jit(solution)/shard_map/pack/pallas_call | solution.py:367
  2.9 1.6 %collective-permute-start.1 = (bf16[256,128]{1,0:T(8,128)(2,1)}, bf16[256,128]{1,0:T(8,128)(2,1)S(1)}, u32[]{:S(2)}, u32[]{:S(2)}) collective-permute-start(bf16[256,128]{1,0:T(8,128)(2,1)} %bitcast.15), channel_id=1, source_target_pairs={{0,1},{1,0},{2,3},{3,2},{4,8},{5,9},{6,10},{7,11},{8,4},{9,5},{10,... | collective-permute-start | bytes 196616 | tf_op jit(solution)/shard_map/ppermute | solution.py:360
  4.6 1.5 %collective-permute-start.2 = (bf16[256,128]{1,0:T(8,128)(2,1)}, bf16[256,128]{1,0:T(8,128)(2,1)S(1)}, u32[]{:S(2)}, u32[]{:S(2)}) collective-permute-start(bf16[256,128]{1,0:T(8,128)(2,1)} %bitcast.17), channel_id=1, source_target_pairs={{0,2},{1,3},{2,0},{3,1},{4,6},{5,7},{6,4},{7,5},{8,10},{9,11},{10,... | collective-permute-start | bytes 196616 | tf_op jit(solution)/shard_map/ppermute | solution.py:363
  6.1 2.0 %collective-permute-start.6 = (bf16[1792,128]{1,0:T(8,128)(2,1)}, bf16[1792,128]{1,0:T(8,128)(2,1)S(1)}, u32[]{:S(2)}, u32[]{:S(2)}) collective-permute-start(bf16[1792,128]{1,0:T(8,128)(2,1)} %bitcast.22), channel_id=1, source_target_pairs={{0,4},{1,5},{2,6},{3,7},{4,0},{5,1},{6,2},{7,3},{8,12},{9,13},{10,... | collective-permute-start | bytes 1376264 | tf_op jit(solution)/shard_map/ppermute | solution.py:360
  8.1 0.4 %collective-permute-start.7 = (bf16[1792,128]{1,0:T(8,128)(2,1)}, bf16[1792,128]{1,0:T(8,128)(2,1)S(1)}, u32[]{:S(2)}, u32[]{:S(2)}) collective-permute-start(bf16[1792,128]{1,0:T(8,128)(2,1)} %bitcast.21), channel_id=1, source_target_pairs={{0,1},{1,0},{2,3},{3,2},{4,8},{5,9},{6,10},{7,11},{8,4},{9,5},{10,... | collective-permute-start | bytes 1376264 | tf_op jit(solution)/shard_map/ppermute | solution.py:360
  8.6 1.2 %collective-permute-done.refs_3_ = bf16[256,128]{1,0:T(8,128)(2,1)S(1)} collective-permute-done((bf16[256,128]{1,0:T(8,128)(2,1)}, bf16[256,128]{1,0:T(8,128)(2,1)S(1)}, u32[]{:S(2)}, u32[]{:S(2)}) %collective-permute-start) | collective-permute-done | bytes 65568 | tf_op jit(solution)/shard_map/ppermute | solution.py:360
  9.8 1.6 %collective-permute-start.4 = (bf16[512,128]{1,0:T(8,128)(2,1)S(1)}, bf16[512,128]{1,0:T(8,128)(2,1)S(1)}, u32[]{:S(2)}, u32[]{:S(2)}) collective-permute-start(bf16[512,128]{1,0:T(8,128)(2,1)S(1)} %pad_maximum_fusion), channel_id=1, source_target_pairs={{0,2},{1,3},{2,0},{3,1},{4,6},{5,7},{6,4},{7,5},{8,10},{9,11},{10,... | collective-permute-start | bytes 393224 | tf_op jit(solution)/shard_map/ppermute | solution.py:363
  11.5 0.8 %copy-done.5 = bf16[32,8,128]{2,1,0:T(8,128)(2,1)S(1)} copy-done((bf16[32,8,128]{2,1,0:T(8,128)(2,1)S(1)}, bf16[32,8,128]{2,1,0:T(8,128)(2,1)}, u32[]{:S(2)}) %copy-start.5) | copy-done | bytes 65560
  12.3 0.7 %copy-done.6 = f32[1,4,256]{2,1,0:T(4,128)S(1)} copy-done((f32[1,4,256]{2,1,0:T(4,128)S(1)}, f32[1,4,256]{2,1,0:T(4,128)}, u32[]{:S(2)}) %copy-start.6) | copy-done | bytes 4120
  13.0 0.7 %copy-done.7 = s32[1,256]{1,0:T(1,128)S(1)} copy-done((s32[1,256]{1,0:T(1,128)S(1)}, s32[1,256]{1,0:T(1,128)}, u32[]{:S(2)}) %copy-start.7) | copy-done | bytes 1048
  13.7 2.0 %receivers.1 = (bf16[256,256]{1,0:T(8,128)(2,1)S(1)}, bf16[256,128]{1,0:T(8,128)(2,1)S(1)}, f32[4,40,32,128]{3,2,1,0:T(8,128)S(1)}, bf16[1024,128]{1,0:T(8,128)(2,1)S(1)}) custom-call(s32[1,256]{1,0:T(1,128)S(1)} %copy-done.7, f32[1,4,256]{2,1,0:T(4,128)S(1)} %copy-done.6, bf16[256,128]{1,0:T(8,128)(2,1)S(1)} %bitcast.18, ...), custom_call_target="tpu_custom_call" | custom-call | flops 2000000000 | bytes 4194304 | tf_op jit(solution)/shard_map/receivers/pallas_call | solution.py:389
  15.6 0.1 collective-permute-start.3
  15.7 0.5 %collective-permute-start.5 = (bf16[512,128]{1,0:T(8,128)(2,1)S(1)}, bf16[512,128]{1,0:T(8,128)(2,1)S(1)}, u32[]{:S(2)}, u32[]{:S(2)}) collective-permute-start(bf16[512,128]{1,0:T(8,128)(2,1)S(1)} %collective-permute-done.4.refs_3_), channel_id=1, source_target_pairs={{0,1},{1,0},{2,3},{3,2},{4,5},{5,4},{6,7},{7,6},{8,9},{9,8},{10,11... | collective-permute-start | bytes 393224 | tf_op jit(solution)/shard_map/ppermute | solution.py:363
  16.8 0.6 %collective-permute-done.5.refs_4_ = bf16[512,128]{1,0:T(8,128)(2,1)S(1)} collective-permute-done((bf16[512,128]{1,0:T(8,128)(2,1)S(1)}, bf16[512,128]{1,0:T(8,128)(2,1)S(1)}, u32[]{:S(2)}, u32[]{:S(2)}) %collective-permute-start.5) | collective-permute-done | bytes 131104 | tf_op jit(solution)/shard_map/ppermute | solution.py:363
  17.4 1.6 %model.1 = (f32[3,48,32,128]{3,2,1,0:T(8,128)S(1)}, f32[48,32,128]{2,1,0:T(8,128)S(1)}, f32[16,32,128]{2,1,0:T(8,128)S(1)}) custom-call(s32[1,2]{1,0:T(1,128)S(1)} %copy-done.4, bf16[1024,128]{1,0:T(8,128)(2,1)S(1)} %get-tuple-element.19.refs_1_, bf16[1024,128]{1,0:T(8,128)(2,1)S(1)} %collective-permute-done.3.refs_2_, ...), custom_call_target="tpu_custom_call" | custom-call | flops 1000000 | bytes 1048576 | tf_op jit(solution)/shard_map/model/pallas_call | solution.py:418
  19.0 0.4 %collective-permute-done.7.refs_14_ = bf16[1792,128]{1,0:T(8,128)(2,1)S(1)} collective-permute-done((bf16[1792,128]{1,0:T(8,128)(2,1)}, bf16[1792,128]{1,0:T(8,128)(2,1)S(1)}, u32[]{:S(2)}, u32[]{:S(2)}) %collective-permute-start.7) | collective-permute-done | bytes 458784 | tf_op jit(solution)/shard_map/ppermute | solution.py:360
  19.5 6.5 %window.1 = (f32[4,128,128]{2,1,0:T(8,128)S(1)}, f32[512,128]{1,0:T(8,128)S(1)}, f32[512,128]{1,0:T(8,128)S(1)}) custom-call(s32[1,2]{1,0:T(1,128)S(1)} %copy-done.4, s32[1]{0:T(128)S(6)} %copy.14.refs_1_, f32[1,4]{1,0:T(1,128)S(1)} %copy-done.8, bf16[256,256]{1,0:T(8,128)(2,1)S(1)} %get-tuple-element.17.refs_5_.refs_3_, ...), custom_call_target="tpu_custom_call" | custom-call | flops 10000000000 | bytes 16777216 | tf_op jit(solution)/shard_map/window/pallas_call | solution.py:442
  26.0 0.1 collective-permute-start.8
  26.1 1.3 %collective-permute-done.8 = f32[2,128,128]{2,1,0:T(8,128)S(1)} collective-permute-done((f32[2,128,128]{2,1,0:T(8,128)S(1)}, f32[2,128,128]{2,1,0:T(8,128)S(1)}, u32[]{:S(2)}, u32[]{:S(2)}) %collective-permute-start.8) | collective-permute-done | bytes 131104 | tf_op jit(solution)/shard_map/ppermute | solution.py:363
  27.4 0.1 collective-permute-start.9
  27.5 0.7 %convert_element_type.6 = bf16[512,128]{1,0:T(8,128)(2,1)} convert(f32[512,128]{1,0:T(8,128)S(1)} %get-tuple-element.27) | non-fusion elementwise | flops 65536 | bytes 393216 | tf_op jit(solution)/shard_map/convert_element_type | solution.py:460
  28.2 0.7 %convert_element_type.7 = bf16[512,128]{1,0:T(8,128)(2,1)} convert(f32[512,128]{1,0:T(8,128)S(1)} %get-tuple-element.28) | non-fusion elementwise | flops 65536 | bytes 393216 | tf_op jit(solution)/shard_map/convert_element_type | solution.py:460
  28.8 2.9 %collective-permute-done.9 = f32[1,128,128]{2,1,0:T(8,128)S(1)} collective-permute-done((f32[1,128,128]{2,1,0:T(8,128)S(1)}, f32[1,128,128]{2,1,0:T(8,128)S(1)}, u32[]{:S(2)}, u32[]{:S(2)}) %collective-permute-start.9) | collective-permute-done | bytes 65568 | tf_op jit(solution)/shard_map/ppermute | solution.py:363
  31.8 0.6 %fusion = f32[16,8,128]{2,1,0:T(8,128)} fusion(f32[1,128,128]{2,1,0:T(8,128)S(1)} %collective-permute-done.9, f32[2,128,128]{2,1,0:T(8,128)S(1)} %slice_add_fusion), kind=kLoop, calls=%fused_computation.3 | loop fusion | flops 16384 | bytes 196608 | tf_op jit(solution)/shard_map/reshape;squeeze | solution.py:459
  (25 shorter events, 0.1 us)
Async XLA Ops:
  2.9 5.6 %collective-permute-start.1 = (bf16[256,128]{1,0:T(8,128)(2,1)}, bf16[256,128]{1,0:T(8,128)(2,1)S(1)}, u32[]{:S(2)}, u32[]{:S(2)}) collective-permute-start(bf16[256,128]{1,0:T(8,128)(2,1)} %bitcast.15), channel_id=1, source_target_pairs={{0,1},{1,0},{2,3},{3,2},{4,8},{5,9},{6,10},{7,11},{8,4},{9,5},{10,... | collective-permute-start | bytes 196616 | tf_op jit(solution)/shard_map/ppermute | solution.py:360
  4.6 5.2 %collective-permute-start = (bf16[256,128]{1,0:T(8,128)(2,1)}, bf16[256,128]{1,0:T(8,128)(2,1)S(1)}, u32[]{:S(2)}, u32[]{:S(2)}) collective-permute-start(bf16[256,128]{1,0:T(8,128)(2,1)} %bitcast.16), channel_id=1, source_target_pairs={{0,4},{1,5},{2,6},{3,7},{4,0},{5,1},{6,2},{7,3},{8,12},{9,13},{10,... | collective-permute-start | bytes 196616 | tf_op jit(solution)/shard_map/ppermute | solution.py:360
  4.6 6.9 %collective-permute-start.2 = (bf16[256,128]{1,0:T(8,128)(2,1)}, bf16[256,128]{1,0:T(8,128)(2,1)S(1)}, u32[]{:S(2)}, u32[]{:S(2)}) collective-permute-start(bf16[256,128]{1,0:T(8,128)(2,1)} %bitcast.17), channel_id=1, source_target_pairs={{0,2},{1,3},{2,0},{3,1},{4,6},{5,7},{6,4},{7,5},{8,10},{9,11},{10,... | collective-permute-start | bytes 196616 | tf_op jit(solution)/shard_map/ppermute | solution.py:363
  6.1 12.9 %collective-permute-start.6 = (bf16[1792,128]{1,0:T(8,128)(2,1)}, bf16[1792,128]{1,0:T(8,128)(2,1)S(1)}, u32[]{:S(2)}, u32[]{:S(2)}) collective-permute-start(bf16[1792,128]{1,0:T(8,128)(2,1)} %bitcast.22), channel_id=1, source_target_pairs={{0,4},{1,5},{2,6},{3,7},{4,0},{5,1},{6,2},{7,3},{8,12},{9,13},{10,... | collective-permute-start | bytes 1376264 | tf_op jit(solution)/shard_map/ppermute | solution.py:360
  8.1 11.3 %collective-permute-start.7 = (bf16[1792,128]{1,0:T(8,128)(2,1)}, bf16[1792,128]{1,0:T(8,128)(2,1)S(1)}, u32[]{:S(2)}, u32[]{:S(2)}) collective-permute-start(bf16[1792,128]{1,0:T(8,128)(2,1)} %bitcast.21), channel_id=1, source_target_pairs={{0,1},{1,0},{2,3},{3,2},{4,8},{5,9},{6,10},{7,11},{8,4},{9,5},{10,... | collective-permute-start | bytes 1376264 | tf_op jit(solution)/shard_map/ppermute | solution.py:360
  9.8 9.7 %copy-start.8 = (f32[1,4]{1,0:T(1,128)S(1)}, f32[1,4]{1,0:T(1,128)}, u32[]{:S(2)}) copy-start(f32[1,4]{1,0:T(1,128)} %refs_2_.3) | copy-start | bytes 52
  9.8 7.6 %copy-start.4 = (s32[1,2]{1,0:T(1,128)S(1)}, s32[1,2]{1,0:T(1,128)}, u32[]{:S(2)}) copy-start(s32[1,2]{1,0:T(1,128)} %refs_0_.7) | copy-start | bytes 28
  9.8 9.7 %copy-start = (bf16[1,16,32,128]{3,2,1,0:T(8,128)(2,1)S(1)}, bf16[1,16,32,128]{3,2,1,0:T(8,128)(2,1)}, u32[]{:S(2)}) copy-start(bf16[1,16,32,128]{3,2,1,0:T(8,128)(2,1)} %refs_2_.2) | copy-start | bytes 393220
  9.8 9.7 %copy-start.1 = (bf16[1,16,32,128]{3,2,1,0:T(8,128)(2,1)S(1)}, bf16[1,16,32,128]{3,2,1,0:T(8,128)(2,1)}, u32[]{:S(2)}) copy-start(bf16[1,16,32,128]{3,2,1,0:T(8,128)(2,1)} %refs_3_.1) | copy-start | bytes 393220
  9.8 9.7 %copy-start.2 = (bf16[1,16,32,128]{3,2,1,0:T(8,128)(2,1)S(1)}, bf16[1,16,32,128]{3,2,1,0:T(8,128)(2,1)}, u32[]{:S(2)}) copy-start(bf16[1,16,32,128]{3,2,1,0:T(8,128)(2,1)} %refs_4_.1) | copy-start | bytes 393220
  9.8 9.7 %copy-start.3 = (bf16[1,16,32,128]{3,2,1,0:T(8,128)(2,1)S(1)}, bf16[1,16,32,128]{3,2,1,0:T(8,128)(2,1)}, u32[]{:S(2)}) copy-start(bf16[1,16,32,128]{3,2,1,0:T(8,128)(2,1)} %refs_5_.1) | copy-start | bytes 393220
  9.8 5.9 %collective-permute-start.4 = (bf16[512,128]{1,0:T(8,128)(2,1)S(1)}, bf16[512,128]{1,0:T(8,128)(2,1)S(1)}, u32[]{:S(2)}, u32[]{:S(2)}) collective-permute-start(bf16[512,128]{1,0:T(8,128)(2,1)S(1)} %pad_maximum_fusion), channel_id=1, source_target_pairs={{0,2},{1,3},{2,0},{3,1},{4,6},{5,7},{6,4},{7,5},{8,10},{9,11},{10,... | collective-permute-start | bytes 393224 | tf_op jit(solution)/shard_map/ppermute | solution.py:363
  11.4 0.8 %copy-start.5 = (bf16[32,8,128]{2,1,0:T(8,128)(2,1)S(1)}, bf16[32,8,128]{2,1,0:T(8,128)(2,1)}, u32[]{:S(2)}) copy-start(bf16[32,8,128]{2,1,0:T(8,128)(2,1)} %get-tuple-element.16) | copy-start | bytes 196612
  12.3 0.7 %copy-start.6 = (f32[1,4,256]{2,1,0:T(4,128)S(1)}, f32[1,4,256]{2,1,0:T(4,128)}, u32[]{:S(2)}) copy-start(f32[1,4,256]{2,1,0:T(4,128)} %refs_1_.4) | copy-start | bytes 12292
  13.0 0.7 %copy-start.7 = (s32[1,256]{1,0:T(1,128)S(1)}, s32[1,256]{1,0:T(1,128)}, u32[]{:S(2)}) copy-start(s32[1,256]{1,0:T(1,128)} %refs_0_.5) | copy-start | bytes 3076
  15.6 1.8 %collective-permute-start.3 = (bf16[1024,128]{1,0:T(8,128)(2,1)S(1)}, bf16[1024,128]{1,0:T(8,128)(2,1)S(1)}, u32[]{:S(2)}, u32[]{:S(2)}) collective-permute-start(bf16[1024,128]{1,0:T(8,128)(2,1)S(1)} %get-tuple-element.19.refs_1_), channel_id=1, source_target_pairs={{0,1},{1,0},{2,3},{3,2},{4,5},{5,4},{6,7},{7,6},{8,9},{9,8},{10,11... | collective-permute-start | bytes 786440 | tf_op jit(solution)/shard_map/ppermute | solution.py:363
  15.7 1.7 %collective-permute-start.5 = (bf16[512,128]{1,0:T(8,128)(2,1)S(1)}, bf16[512,128]{1,0:T(8,128)(2,1)S(1)}, u32[]{:S(2)}, u32[]{:S(2)}) collective-permute-start(bf16[512,128]{1,0:T(8,128)(2,1)S(1)} %collective-permute-done.4.refs_3_), channel_id=1, source_target_pairs={{0,1},{1,0},{2,3},{3,2},{4,5},{5,4},{6,7},{7,6},{8,9},{9,8},{10,11... | collective-permute-start | bytes 393224 | tf_op jit(solution)/shard_map/ppermute | solution.py:363
  26.0 1.4 %collective-permute-start.8 = (f32[2,128,128]{2,1,0:T(8,128)S(1)}, f32[2,128,128]{2,1,0:T(8,128)S(1)}, u32[]{:S(2)}, u32[]{:S(2)}) collective-permute-start(f32[2,128,128]{2,1,0:T(8,128)S(1)} %slice.13), channel_id=1, source_target_pairs={{0,1},{1,0},{2,3},{3,2},{4,5},{5,4},{6,7},{7,6},{8,9},{9,8},{10,11... | collective-permute-start | bytes 393224 | tf_op jit(solution)/shard_map/ppermute | solution.py:363
  27.4 4.3 %collective-permute-start.9 = (f32[1,128,128]{2,1,0:T(8,128)S(1)}, f32[1,128,128]{2,1,0:T(8,128)S(1)}, u32[]{:S(2)}, u32[]{:S(2)}) collective-permute-start(f32[1,128,128]{2,1,0:T(8,128)S(1)} %slice.17), channel_id=1, source_target_pairs={{0,2},{1,3},{2,0},{3,1},{4,6},{5,7},{6,4},{7,5},{8,10},{9,11},{10,... | collective-permute-start | bytes 196616 | tf_op jit(solution)/shard_map/ppermute | solution.py:363

commit v2 on v1

--- a/solution.py
+++ b/solution.py
@@ -66,26 +66,38 @@
 
 
 def pack_kernel(*refs):
-    velocity_ref, density_ref, now_ref, before_ref, end_ref, after_ref, model_ref, a_ref, b_ref, sems = refs
+    (velocity_ref, density_ref, now_ref, before_ref, end_ref, after_ref, model_ref, a_ref, b_ref, model_buf, now_buf, before_buf,
+     end_buf, after_buf, in_sems, out_sems) = refs
     cx = velocity_ref.shape[0]
     even = lax.rem(lax.axis_index("tile"), 2) == 0
     reach = (STEPS - 1) * HALO
-    moves = [(velocity_ref, model_ref.at[0:cx]), (density_ref, model_ref.at[cx : 2 * cx])]
+    loads = [
+        (velocity_ref, model_buf.at[0:cx]), (density_ref, model_buf.at[cx : 2 * cx]), (now_ref.at[0], now_buf),
+        (before_ref.at[0], before_buf), (end_ref.at[0], end_buf), (after_ref.at[0], after_buf),
+    ]
+    loads = [pltpu.make_async_copy(src, dst, in_sems.at[number]) for number, (src, dst) in enumerate(loads)]
+    for load in loads:
+        load.start()
+    stores = [[], [(model_buf, model_ref)], [], [], [], []]
     for side, out_ref in enumerate((a_ref, b_ref)):
         first = jnp.where(even == (side == 0), cx - reach, 0)
         base = 0
-        for whole_ref, part_ref in ((now_ref, before_ref), (end_ref, after_ref)):
-            moves.append((whole_ref.at[0], out_ref.at[base : base + cx]))
-            moves.append((part_ref.at[0, pl.ds(first, reach)], out_ref.at[base + cx : base + cx + reach]))
+        for number, (whole, part) in ((2, (now_buf, before_buf)), (4, (end_buf, after_buf))):
+            stores[number].append((whole, out_ref.at[base : base + cx]))
+            stores[number + 1].append((part.at[pl.ds(first, reach)], out_ref.at[base + cx : base + cx + reach]))
             base += cx + reach
-    copies = [pltpu.make_async_copy(src, dst, sems.at[number]) for number, (src, dst) in enumerate(moves)]
-    for copy in copies:
-        copy.start()
-    for copy in copies:
+    started = []
+    for load, after in zip(loads, stores):
+        load.wait()
+        for src, dst in after:
+            copy = pltpu.make_async_copy(src, dst, out_sems.at[len(started)])
+            copy.start()
+            started.append(copy)
+    for copy in started:
         copy.wait()
 
 
-def setup_kernel(cx, cells_ref, traces_ref, *refs):
+def setup_kernel(cx, receivers_ref, *refs):
     parts, (along_z_ref, along_y_ref, add_ref, joined_ref) = refs[:-4], refs[-4:]
     ny, nz = add_ref.shape[2:]
     size = parts[0].shape[0]
@@ -103,16 +115,16 @@
     along_y_ref[...] = jnp.where(here, jnp.where(rows < shape[1], first, second), 0.0).astype(jnp.bfloat16)
 
     tile = lax.axis_index("tile")
-    count = cells_ref.shape[1]
-    cells = cells_ref[...]
+    count = receivers_ref.shape[1]
+    cells = receivers_ref[STEPS : STEPS + 1, :].astype(jnp.int32)
     reach = (STEPS - 1) * HALO
     at_row = cells // nz - (tile * cx - reach) * ny
     at_z = lax.rem(cells, nz)
     depth = lax.broadcasted_iota(jnp.int32, (nz, count), 0)
     deep = depth == at_z
     tile = lax.axis_index("tile")
-    count = cells_ref.shape[1]
-    cells = cells_ref[...]
+    count = receivers_ref.shape[1]
+    cells = receivers_ref[STEPS : STEPS + 1, :].astype(jnp.int32)
     reach = (STEPS - 1) * HALO
     at_row = cells // nz - (tile * cx - reach) * ny
     at_z = lax.rem(cells, nz)
@@ -120,7 +132,7 @@
     deep = depth == at_z
     values = []
     for step in range(STEPS):
-        trace = traces_ref[0, pl.ds(STEPS - 1 - step, 1), :]
+        trace = receivers_ref[pl.ds(STEPS - 1 - step, 1), :]
         high = trace.astype(jnp.bfloat16).astype(jnp.float32)
         values += [jnp.where(deep, high, 0.0), jnp.where(deep, trace - high, 0.0)]
     values = jnp.concatenate(values, axis=0).astype(jnp.bfloat16)
@@ -157,15 +169,12 @@
     return first_y.reshape(shape), first_z.reshape(shape), jnp.concatenate(second, axis=0).reshape(shape)
 
 
-def layer_differences(buf, i, summed):
+def first_along_x(buf, i):
     first = None
     for k in range(1, 5):
-        plus, minus = buf[i + k], buf[i - k]
-        if summed is not None:
-            summed = summed + SECOND[k - 1] * (plus + minus)
-        term = FIRST[k - 1] * (plus - minus)
+        term = FIRST[k - 1] * (buf[i + k] - buf[i - k])
         first = term if first is None else first + term
-    return first, summed
+    return first
 
 
 def on_segments(step, left, right, cx, work):
@@ -181,17 +190,21 @@
         lax.fori_loop(0, left.astype(jnp.int32) + right.astype(jnp.int32), body, 0)
 
 
-def march(pairs, slopes_ref, courant_ref, along_z, along_y, i0, layers, use):
+def march(pairs, ahead_ref, slopes_ref, courant_ref, along_z, along_y, i0, layers, use):
     parts = [matrix_differences(cur, i0, layers, along_z, along_y) for cur, _ in pairs]
     for j in range(layers):
         i = i0 + j
-        slopes = [slopes_ref[axis, i] for axis in range(3)]
+        applied = [second[j] for _, _, second in parts]
+        for k in range(1, 5):
+            for side, offset in enumerate((k, -k)):
+                factor = ahead_ref[2 * (k - 1) + side, i]
+                applied = [value + factor * cur[i + offset] for value, (cur, _) in zip(applied, pairs)]
+        along = [slopes_ref[axis, i] for axis in range(2)]
         courant = courant_ref[i]
         steps = []
-        for (cur, prev), (first_y, first_z, second) in zip(pairs, parts):
-            first_x, applied = layer_differences(cur, i, second[j])
-            applied = applied - slopes[0] * first_x - slopes[1] * first_y[j] - slopes[2] * first_z[j]
-            steps.append((applied, 2.0 * cur[i] - prev[i] + courant * applied))
+        for value, (cur, prev), (first_y, first_z, _) in zip(applied, pairs, parts):
+            value = value - along[0] * first_y[j] - along[1] * first_z[j]
+            steps.append((value, 2.0 * cur[i] - prev[i] + courant * value))
         for (_, prev), updated in zip(pairs, use(i, j, steps)):
             prev[i] = updated
 
@@ -227,7 +240,7 @@
 
 def model_kernel(cx, ny, nz, shots, blocks, aperture_ref, *refs):
     model_refs = refs[: len(blocks)]
-    along_z_ref, along_y_ref, slopes_ref, courant_ref, gain_ref, log_buf = refs[len(blocks) :]
+    along_z_ref, along_y_ref, ahead_ref, slopes_ref, courant_ref, gain_ref, log_buf = refs[len(blocks) :]
     tile, own, left, right, side_a, side_b = layout(aperture_ref, cx)
     shot = lax.axis_index("shot")
     sides = ((cx, None), (side_a[0], side_a[1]), (side_b[0], side_b[1]))
@@ -256,15 +269,19 @@
         def slopes(i0, layers, inner):
             first_y, first_z, _ = matrix_differences(log_buf, i0, layers, along_z, along_y)
             for j in range(layers):
-                slopes_ref[0, i0 + j] = layer_differences(log_buf, i0 + j, None)[0] * (1.0 / 140.0)
-                slopes_ref[1, i0 + j] = first_y[j] * (1.0 / 140.0)
-                slopes_ref[2, i0 + j] = first_z[j] * (1.0 / 140.0)
+                i = i0 + j
+                along_x = first_along_x(log_buf, i) * (1.0 / 140.0)
+                for k in range(1, 5):
+                    ahead_ref[2 * k - 2, i] = SECOND[k - 1] - FIRST[k - 1] * along_x
+                    ahead_ref[2 * k - 1, i] = SECOND[k - 1] + FIRST[k - 1] * along_x
+                slopes_ref[0, i] = first_y[j] * (1.0 / 140.0)
+                slopes_ref[1, i] = first_z[j] * (1.0 / 140.0)
 
         on_segments(0, left, right, cx, slopes)
 
 
 def window_kernel(
-    cx, ny, nz, order, aperture_ref, source_ref, wavelet_ref, along_z_ref, along_y_ref, slopes_ref, courant_ref, gain_ref, add_ref,
+    cx, ny, nz, order, aperture_ref, source_ref, wavelet_ref, along_z_ref, along_y_ref, ahead_ref, slopes_ref, courant_ref, gain_ref, add_ref,
     now_ref, before_ref, end_ref, after_ref, from_a, from_b, sums_ref, wave_ref, adjoint_ref, now, before, end, after, applied_held,
     adjoint_held, image,
 ):
@@ -306,7 +323,7 @@
                         image[j] = terms if 2 * step == STEPS else image[j] + terms
                     return wave, back
 
-                march(here, slopes_ref, courant_ref, along_z, along_y, i0, layers, use)
+                march(here, ahead_ref, slopes_ref, courant_ref, along_z, along_y, i0, layers, use)
 
             on_segments(step, left, right, cx, work)
             reach = (STEPS - 1 - step) * HALO
@@ -368,8 +385,10 @@
         pack_kernel,
         out_shape=(jax.ShapeDtypeStruct((2 * cx,) + velocity.shape[1:], jnp.bfloat16), message, message),
         in_specs=[pl.BlockSpec(memory_space=pltpu.HBM)] * 6,
-        out_specs=(vmem(),) * 3,
-        scratch_shapes=[pltpu.SemaphoreType.DMA((10,))],
+        out_specs=(pl.BlockSpec(memory_space=pltpu.HBM),) * 3,
+        scratch_shapes=[pltpu.VMEM((2 * cx,) + velocity.shape[1:], jnp.bfloat16)]
+        + [pltpu.VMEM((cx, ny, nz), jnp.bfloat16)] * 4
+        + [pltpu.SemaphoreType.DMA((6,)), pltpu.SemaphoreType.DMA((9,))],
         compiler_params=pltpu.CompilerParams(vmem_limit_bytes=PACK_BYTES),
         cost_estimate=pl.CostEstimate(flops=0, bytes_accessed=2 * 2**20, transcendentals=0),
         name="pack",
@@ -383,9 +402,10 @@
     near = [([(0, 0)], model), ([(0, 1)], model_a), ([(0, 2)], model_b)]
     late = []
     if high:
-        near.append(([(high, 0)], cross(model, high)))
         late.append(([(high, 1), (high, 2)], cross(jnp.concatenate([model_a, model_b], axis=0), high)))
-
+        late.append(([(high, 0)], cross(model, high)))
+
+    receivers = jnp.concatenate([residual_traces[0], receiver_cell.astype(jnp.float32)], axis=0)
     along_z, along_y, added, joined = pl.pallas_call(
         lambda *refs: setup_kernel(cx, *refs),
         out_shape=(
@@ -394,12 +414,12 @@
             jax.ShapeDtypeStruct((STEPS, cx + 2 * (STEPS - 1) * HALO, ny, nz), jnp.float32),
             jax.ShapeDtypeStruct((len(near) * model.shape[0], nz), jnp.bfloat16),
         ),
-        in_specs=[vmem()] * (2 + len(near)),
+        in_specs=[vmem()] * (1 + len(near)),
         out_specs=(vmem(),) * 4,
         compiler_params=params,
         cost_estimate=pl.CostEstimate(flops=2 * 10**9, bytes_accessed=4 * 2**20, transcendentals=0),
         name="receivers",
-    )(receiver_cell, residual_traces, *[block for _, block in near])
+    )(receivers, *[block for _, block in near])
 
     near = [([name for names, _ in near for name in names], joined)]
     mask = high // 2
@@ -415,15 +435,16 @@
 
     field = pltpu.VMEM((3 * cx, ny, nz), jnp.float32)
     blocks = tuple(tuple(names) for names, _ in held)
-    slopes, courant, gain = pl.pallas_call(
+    ahead, slopes, courant, gain = pl.pallas_call(
         lambda *refs: model_kernel(cx, ny, nz, shots, blocks, *refs),
         out_shape=(
-            jax.ShapeDtypeStruct((3, 3 * cx, ny, nz), jnp.float32),
+            jax.ShapeDtypeStruct((8, 3 * cx, ny, nz), jnp.float32),
+            jax.ShapeDtypeStruct((2, 3 * cx, ny, nz), jnp.float32),
             jax.ShapeDtypeStruct((3 * cx, ny, nz), jnp.float32),
             jax.ShapeDtypeStruct((cx, ny, nz), jnp.float32),
         ),
         in_specs=[smem()] + [vmem()] * (len(held) + 2),
-        out_specs=(vmem(),) * 3,
+        out_specs=(vmem(),) * 4,
         scratch_shapes=[field],
         compiler_params=params,
         cost_estimate=pl.CostEstimate(flops=10**6, bytes_accessed=2**20, transcendentals=0),
@@ -446,13 +467,13 @@
             jax.ShapeDtypeStruct((rows, nz), jnp.float32),
             jax.ShapeDtypeStruct((rows, nz), jnp.float32),
         ),
-        in_specs=[smem()] * 3 + [vmem()] * 12,
+        in_specs=[smem()] * 3 + [vmem()] * 13,
         out_specs=(vmem(),) * 3,
         scratch_shapes=[field] * 4 + [pltpu.VMEM((STEPS // 2, cx, ny, nz), jnp.float32)] * 2 + [pltpu.VMEM((cx, ny, nz), jnp.float32)],
         compiler_params=params,
         cost_estimate=pl.CostEstimate(flops=10**10, bytes_accessed=16 * 2**20, transcendentals=0),
         name="window",
-    )(aperture, source_cell, source_wave, along_z, along_y, slopes, courant, gain, added, *fields, from_a, from_b)
+    )(aperture, source_cell, source_wave, along_z, along_y, ahead, slopes, courant, gain, added, *fields, from_a, from_b)
     for bit in bits:
         half = sums.shape[0] // 2
         sums = sums[:half] + cross(sums[half:], bit)

time: 32.4 us -> 33.7 us (1.040)
  the two profiles are of different devices: /device:TPU:8 before, /device:TPU:16 now
where the time goes in v2:
time: 33.7 us; the launch traced here: 33.2 us
  Pallas kernels  13.5 us (40%)
  starting transfers between devices  7.03 us (21%)
  waiting for transfers between devices  6.92 us (21%)
  other arithmetic  3.39 us (10%)
  between operations  1.46 us (4%)
  local copies, waits for them, and re-layouts  0.89 us (3%)
    pallas_call x1, Pallas kernels, local(): pl.pallas_call(lambda *refs: window_kernel(cx, ny, nz, order, *refs), out...  7.75 us
    ppermute x6, waiting for transfers between devices, cross(): return lax.ppermute(x, 'shot', [(i, i ^ mask) for i in range(shots)])  6.03 us
    ppermute x4, starting transfers between devices, swap(): return lax.ppermute(x, ('tile', 'shot'), pairs((tiles, shots), kind))  4.05 us
    ppermute x6, starting transfers between devices, cross(): return lax.ppermute(x, 'shot', [(i, i ^ mask) for i in range(shots)])  2.98 us
    pallas_call x1, Pallas kernels, local(): pl.pallas_call(pack_kernel, out_shape=(jax.ShapeDtypeStruct((2 * cx,) + v...  1.98 us
    pallas_call x1, Pallas kernels, local(): pl.pallas_call(lambda *refs: setup_kernel(cx, *refs), out_shape=(jax.Shap...  1.95 us
    pallas_call x1, Pallas kernels, local(): pl.pallas_call(lambda *refs: model_kernel(cx, ny, nz, shots, blocks, *ref...  1.78 us
    convert_element_type x2, other arithmetic, local(): x.astype(jnp.bfloat16).reshape(wave_now.shape)  1.34 us
  transfers between devices with their start and end apart: 10, of which 5 were waited for; matrix products, arithmetic and copies ran while one was open for 8% of the time, Pallas kernels for 11%

profile of v2, /device:TPU:16, one launch (start us, length us, event | category | flops | bytes accessed | tf_op | source)
XLA Modules:
  0.0 33.2 jit_solution(6302869679782285521)
XLA Ops:
  0.6 2.0 %pack.1 = (bf16[32,8,128]{2,1,0:T(8,128)(2,1)}, bf16[56,32,128]{2,1,0:T(8,128)(2,1)}, bf16[56,32,128]{2,1,0:T(8,128)(2,1)}) custom-call(bf16[16,8,128]{2,1,0:T(8,128)(2,1)} %refs_0_.3, bf16[16,8,128]{2,1,0:T(8,128)(2,1)} %refs_1_.2, bf16[1,16,32,128]{3,2,1,0:T(8,128)(2,1)} %refs_2_.2, bf16[1,16,32,128]{3,2,1,0:T(8,128)(2,1)} %refs_3_.1, ...), custom_call_target="tpu_custom_call" | custom-call | bytes 2097152 | tf_op jit(solution)/shard_map/pack/pallas_call | solution.py:384
  2.6 1.6 %collective-permute-start.4 = (bf16[256,128]{1,0:T(8,128)(2,1)}, bf16[256,128]{1,0:T(8,128)(2,1)S(1)}, u32[]{:S(2)}, u32[]{:S(2)}) collective-permute-start(bf16[256,128]{1,0:T(8,128)(2,1)} %bitcast.16), channel_id=1, source_target_pairs={{0,2},{1,3},{2,0},{3,1},{4,6},{5,7},{6,4},{7,5},{8,10},{9,11},{10,... | collective-permute-start | bytes 196616 | tf_op jit(solution)/shard_map/ppermute | solution.py:380
  4.2 0.4 %collective-permute-start.1 = (bf16[256,128]{1,0:T(8,128)(2,1)}, bf16[256,128]{1,0:T(8,128)(2,1)S(1)}, u32[]{:S(2)}, u32[]{:S(2)}) collective-permute-start(bf16[256,128]{1,0:T(8,128)(2,1)} %bitcast.17), channel_id=1, source_target_pairs={{0,1},{1,0},{2,3},{3,2},{4,8},{5,9},{6,10},{7,11},{8,4},{9,5},{10,... | collective-permute-start | bytes 196616 | tf_op jit(solution)/shard_map/ppermute | solution.py:377
  4.6 1.1 %collective-permute-start = (bf16[256,128]{1,0:T(8,128)(2,1)}, bf16[256,128]{1,0:T(8,128)(2,1)S(1)}, u32[]{:S(2)}, u32[]{:S(2)}) collective-permute-start(bf16[256,128]{1,0:T(8,128)(2,1)} %bitcast.18), channel_id=1, source_target_pairs={{0,4},{1,5},{2,6},{3,7},{4,0},{5,1},{6,2},{7,3},{8,12},{9,13},{10,... | collective-permute-start | bytes 196616 | tf_op jit(solution)/shard_map/ppermute | solution.py:377
  5.8 0.9 %collective-permute-start.6 = (bf16[1792,128]{1,0:T(8,128)(2,1)}, bf16[1792,128]{1,0:T(8,128)(2,1)S(1)}, u32[]{:S(2)}, u32[]{:S(2)}) collective-permute-start(bf16[1792,128]{1,0:T(8,128)(2,1)} %bitcast.24), channel_id=1, source_target_pairs={{0,4},{1,5},{2,6},{3,7},{4,0},{5,1},{6,2},{7,3},{8,12},{9,13},{10,... | collective-permute-start | bytes 1376264 | tf_op jit(solution)/shard_map/ppermute | solution.py:377
  6.7 1.6 %collective-permute-start.7 = (bf16[1792,128]{1,0:T(8,128)(2,1)}, bf16[1792,128]{1,0:T(8,128)(2,1)S(1)}, u32[]{:S(2)}, u32[]{:S(2)}) collective-permute-start(bf16[1792,128]{1,0:T(8,128)(2,1)} %bitcast.23), channel_id=1, source_target_pairs={{0,1},{1,0},{2,3},{3,2},{4,8},{5,9},{6,10},{7,11},{8,4},{9,5},{10,... | collective-permute-start | bytes 1376264 | tf_op jit(solution)/shard_map/ppermute | solution.py:377
  8.2 0.7 %convert_element_type.9 = f32[1,256]{1,0:T(1,128)S(1)} convert(s32[1,256]{1,0:T(1,128)} %param.19) | non-fusion elementwise | flops 256 | bytes 2048 | tf_op jit(solution)/shard_map/convert_element_type | solution.py:408
  8.9 0.7 %pad_maximum_fusion.2.refs_0_ = f32[5,256]{1,0:T(8,128)S(1)} fusion(f32[1,256]{1,0:T(1,128)S(1)} %convert_element_type.9, f32[4,256]{1,0:T(4,128)} %bitcast.22), kind=kLoop, calls=%fused_computation.5 | loop fusion | flops 1280 | bytes 10240 | tf_op jit(solution)/shard_map/concatenate | solution.py:408
  9.7 0.6 %collective-permute-start.3 = (bf16[512,128]{1,0:T(8,128)(2,1)S(1)}, bf16[512,128]{1,0:T(8,128)(2,1)S(1)}, u32[]{:S(2)}, u32[]{:S(2)}) collective-permute-start(bf16[512,128]{1,0:T(8,128)(2,1)S(1)} %pad_maximum_fusion.1), channel_id=1, source_target_pairs={{0,2},{1,3},{2,0},{3,1},{4,6},{5,7},{6,4},{7,5},{8,10},{9,11},{10,... | collective-permute-start | bytes 393224 | tf_op jit(solution)/shard_map/ppermute | solution.py:380
  10.3 0.8 %copy-done.5 = bf16[32,8,128]{2,1,0:T(8,128)(2,1)S(1)} copy-done((bf16[32,8,128]{2,1,0:T(8,128)(2,1)S(1)}, bf16[32,8,128]{2,1,0:T(8,128)(2,1)}, u32[]{:S(2)}) %copy-start.5) | copy-done | bytes 65560
  11.1 1.9 %receivers.1 = (bf16[256,256]{1,0:T(8,128)(2,1)S(1)}, bf16[256,128]{1,0:T(8,128)(2,1)S(1)}, f32[4,40,32,128]{3,2,1,0:T(8,128)S(1)}, bf16[768,128]{1,0:T(8,128)(2,1)S(1)}) custom-call(f32[5,256]{1,0:T(8,128)S(1)} %pad_maximum_fusion.2.refs_0_, bf16[256,128]{1,0:T(8,128)(2,1)S(1)} %bitcast.19, bf16[256,128]{1,0:T(8,128)(2,1)S(1)} %collective-permute-done.refs_2_, ...), custom_call_target="tpu_custom_call" | custom-call | flops 2000000000 | bytes 4194304 | tf_op jit(solution)/shard_map/receivers/pallas_call | solution.py:409
  13.1 0.1 collective-permute-start.2
  13.2 1.5 %collective-permute-done.3.refs_3_ = bf16[512,128]{1,0:T(8,128)(2,1)S(1)} collective-permute-done((bf16[512,128]{1,0:T(8,128)(2,1)S(1)}, bf16[512,128]{1,0:T(8,128)(2,1)S(1)}, u32[]{:S(2)}, u32[]{:S(2)}) %collective-permute-start.3) | collective-permute-done | bytes 131104 | tf_op jit(solution)/shard_map/ppermute | solution.py:380
  15.5 0.8 %collective-permute-done.5.refs_5_ = bf16[768,128]{1,0:T(8,128)(2,1)S(1)} collective-permute-done((bf16[768,128]{1,0:T(8,128)(2,1)S(1)}, bf16[768,128]{1,0:T(8,128)(2,1)S(1)}, u32[]{:S(2)}, u32[]{:S(2)}) %collective-permute-start.5) | collective-permute-done | bytes 196640 | tf_op jit(solution)/shard_map/ppermute | solution.py:380
  16.3 1.8 %model.1 = (f32[8,48,32,128]{3,2,1,0:T(8,128)S(1)}, f32[2,48,32,128]{3,2,1,0:T(8,128)S(1)}, f32[48,32,128]{2,1,0:T(8,128)S(1)}, f32[16,32,128]{2,1,0:T(8,128)S(1)}) custom-call(s32[1,2]{1,0:T(1,128)S(1)} %copy-done.4, bf16[768,128]{1,0:T(8,128)(2,1)S(1)} %get-tuple-element.20.refs_1_, bf16[768,128]{1,0:T(8,128)(2,1)S(1)} %collective-permute-done.2.refs_2_, ...), custom_call_target="tpu_custom_call" | custom-call | flops 1000000 | bytes 1048576 | tf_op jit(solution)/shard_map/model/pallas_call | solution.py:438
  18.1 0.9 %collective-permute-done.6.refs_14_ = bf16[1792,128]{1,0:T(8,128)(2,1)S(1)} collective-permute-done((bf16[1792,128]{1,0:T(8,128)(2,1)}, bf16[1792,128]{1,0:T(8,128)(2,1)S(1)}, u32[]{:S(2)}, u32[]{:S(2)}) %collective-permute-start.6) | collective-permute-done | bytes 458784 | tf_op jit(solution)/shard_map/ppermute | solution.py:377
  19.0 7.8 %window.1 = (f32[4,128,128]{2,1,0:T(8,128)S(1)}, f32[512,128]{1,0:T(8,128)S(1)}, f32[512,128]{1,0:T(8,128)S(1)}) custom-call(s32[1,2]{1,0:T(1,128)S(1)} %copy-done.4, s32[1]{0:T(128)S(6)} %copy.14.refs_1_, f32[1,4]{1,0:T(1,128)S(1)} %copy-done.6, bf16[256,256]{1,0:T(8,128)(2,1)S(1)} %get-tuple-element.18.refs_6_.refs_3_, ...), custom_call_target="tpu_custom_call" | custom-call | flops 10000000000 | bytes 16777216 | tf_op jit(solution)/shard_map/window/pallas_call | solution.py:463
  26.8 0.1 collective-permute-start.8
  26.8 1.3 %collective-permute-done.8 = f32[2,128,128]{2,1,0:T(8,128)S(1)} collective-permute-done((f32[2,128,128]{2,1,0:T(8,128)S(1)}, f32[2,128,128]{2,1,0:T(8,128)S(1)}, u32[]{:S(2)}, u32[]{:S(2)}) %collective-permute-start.8) | collective-permute-done | bytes 131104 | tf_op jit(solution)/shard_map/ppermute | solution.py:380
  28.2 0.6 %collective-permute-start.9 = (f32[1,128,128]{2,1,0:T(8,128)S(1)}, f32[1,128,128]{2,1,0:T(8,128)S(1)}, u32[]{:S(2)}, u32[]{:S(2)}) collective-permute-start(f32[1,128,128]{2,1,0:T(8,128)S(1)} %slice.17), channel_id=1, source_target_pairs={{0,2},{1,3},{2,0},{3,1},{4,6},{5,7},{6,4},{7,5},{8,10},{9,11},{10,... | collective-permute-start | bytes 196616 | tf_op jit(solution)/shard_map/ppermute | solution.py:380
  28.8 0.7 %convert_element_type.10 = bf16[512,128]{1,0:T(8,128)(2,1)} convert(f32[512,128]{1,0:T(8,128)S(1)} %get-tuple-element.29) | non-fusion elementwise | flops 65536 | bytes 393216 | tf_op jit(solution)/shard_map/convert_element_type | solution.py:481
  29.5 0.7 %convert_element_type.11 = bf16[512,128]{1,0:T(8,128)(2,1)} convert(f32[512,128]{1,0:T(8,128)S(1)} %get-tuple-element.30) | non-fusion elementwise | flops 65536 | bytes 393216 | tf_op jit(solution)/shard_map/convert_element_type | solution.py:481
  30.2 2.4 %collective-permute-done.9 = f32[1,128,128]{2,1,0:T(8,128)S(1)} collective-permute-done((f32[1,128,128]{2,1,0:T(8,128)S(1)}, f32[1,128,128]{2,1,0:T(8,128)S(1)}, u32[]{:S(2)}, u32[]{:S(2)}) %collective-permute-start.9) | collective-permute-done | bytes 65568 | tf_op jit(solution)/shard_map/ppermute | solution.py:380
  32.5 0.6 %fusion = f32[16,8,128]{2,1,0:T(8,128)} fusion(f32[1,128,128]{2,1,0:T(8,128)S(1)} %collective-permute-done.9, f32[2,128,128]{2,1,0:T(8,128)S(1)} %slice_add_fusion), kind=kLoop, calls=%fused_computation.4 | loop fusion | flops 16384 | bytes 196608 | tf_op jit(solution)/shard_map/reshape;squeeze | solution.py:480
  (24 shorter events, 0.2 us)
Async XLA Ops:
  2.6 10.6 %collective-permute-start.4 = (bf16[256,128]{1,0:T(8,128)(2,1)}, bf16[256,128]{1,0:T(8,128)(2,1)S(1)}, u32[]{:S(2)}, u32[]{:S(2)}) collective-permute-start(bf16[256,128]{1,0:T(8,128)(2,1)} %bitcast.16), channel_id=1, source_target_pairs={{0,2},{1,3},{2,0},{3,1},{4,6},{5,7},{6,4},{7,5},{8,10},{9,11},{10,... | collective-permute-start | bytes 196616 | tf_op jit(solution)/shard_map/ppermute | solution.py:380
  4.2 5.4 %collective-permute-start.1 = (bf16[256,128]{1,0:T(8,128)(2,1)}, bf16[256,128]{1,0:T(8,128)(2,1)S(1)}, u32[]{:S(2)}, u32[]{:S(2)}) collective-permute-start(bf16[256,128]{1,0:T(8,128)(2,1)} %bitcast.17), channel_id=1, source_target_pairs={{0,1},{1,0},{2,3},{3,2},{4,8},{5,9},{6,10},{7,11},{8,4},{9,5},{10,... | collective-permute-start | bytes 196616 | tf_op jit(solution)/shard_map/ppermute | solution.py:377
  4.6 5.0 %collective-permute-start = (bf16[256,128]{1,0:T(8,128)(2,1)}, bf16[256,128]{1,0:T(8,128)(2,1)S(1)}, u32[]{:S(2)}, u32[]{:S(2)}) collective-permute-start(bf16[256,128]{1,0:T(8,128)(2,1)} %bitcast.18), channel_id=1, source_target_pairs={{0,4},{1,5},{2,6},{3,7},{4,0},{5,1},{6,2},{7,3},{8,12},{9,13},{10,... | collective-permute-start | bytes 196616 | tf_op jit(solution)/shard_map/ppermute | solution.py:377
  5.8 13.2 %collective-permute-start.6 = (bf16[1792,128]{1,0:T(8,128)(2,1)}, bf16[1792,128]{1,0:T(8,128)(2,1)S(1)}, u32[]{:S(2)}, u32[]{:S(2)}) collective-permute-start(bf16[1792,128]{1,0:T(8,128)(2,1)} %bitcast.24), channel_id=1, source_target_pairs={{0,4},{1,5},{2,6},{3,7},{4,0},{5,1},{6,2},{7,3},{8,12},{9,13},{10,... | collective-permute-start | bytes 1376264 | tf_op jit(solution)/shard_map/ppermute | solution.py:377
  6.7 12.3 %collective-permute-start.7 = (bf16[1792,128]{1,0:T(8,128)(2,1)}, bf16[1792,128]{1,0:T(8,128)(2,1)S(1)}, u32[]{:S(2)}, u32[]{:S(2)}) collective-permute-start(bf16[1792,128]{1,0:T(8,128)(2,1)} %bitcast.23), channel_id=1, source_target_pairs={{0,1},{1,0},{2,3},{3,2},{4,8},{5,9},{6,10},{7,11},{8,4},{9,5},{10,... | collective-permute-start | bytes 1376264 | tf_op jit(solution)/shard_map/ppermute | solution.py:377
  9.6 6.6 %copy-start.4 = (s32[1,2]{1,0:T(1,128)S(1)}, s32[1,2]{1,0:T(1,128)}, u32[]{:S(2)}) copy-start(s32[1,2]{1,0:T(1,128)} %refs_0_.5) | copy-start | bytes 28
  9.7 9.3 %copy-start = (bf16[1,16,32,128]{3,2,1,0:T(8,128)(2,1)S(1)}, bf16[1,16,32,128]{3,2,1,0:T(8,128)(2,1)}, u32[]{:S(2)}) copy-start(bf16[1,16,32,128]{3,2,1,0:T(8,128)(2,1)} %refs_2_.2) | copy-start | bytes 393220
  9.7 9.3 %copy-start.1 = (bf16[1,16,32,128]{3,2,1,0:T(8,128)(2,1)S(1)}, bf16[1,16,32,128]{3,2,1,0:T(8,128)(2,1)}, u32[]{:S(2)}) copy-start(bf16[1,16,32,128]{3,2,1,0:T(8,128)(2,1)} %refs_3_.1) | copy-start | bytes 393220
  9.7 9.3 %copy-start.2 = (bf16[1,16,32,128]{3,2,1,0:T(8,128)(2,1)S(1)}, bf16[1,16,32,128]{3,2,1,0:T(8,128)(2,1)}, u32[]{:S(2)}) copy-start(bf16[1,16,32,128]{3,2,1,0:T(8,128)(2,1)} %refs_4_.1) | copy-start | bytes 393220
  9.7 9.3 %copy-start.3 = (bf16[1,16,32,128]{3,2,1,0:T(8,128)(2,1)S(1)}, bf16[1,16,32,128]{3,2,1,0:T(8,128)(2,1)}, u32[]{:S(2)}) copy-start(bf16[1,16,32,128]{3,2,1,0:T(8,128)(2,1)} %refs_5_.1) | copy-start | bytes 393220
  9.7 5.0 %collective-permute-start.3 = (bf16[512,128]{1,0:T(8,128)(2,1)S(1)}, bf16[512,128]{1,0:T(8,128)(2,1)S(1)}, u32[]{:S(2)}, u32[]{:S(2)}) collective-permute-start(bf16[512,128]{1,0:T(8,128)(2,1)S(1)} %pad_maximum_fusion.1), channel_id=1, source_target_pairs={{0,2},{1,3},{2,0},{3,1},{4,6},{5,7},{6,4},{7,5},{8,10},{9,11},{10,... | collective-permute-start | bytes 393224 | tf_op jit(solution)/shard_map/ppermute | solution.py:380
  10.3 0.8 %copy-start.5 = (bf16[32,8,128]{2,1,0:T(8,128)(2,1)S(1)}, bf16[32,8,128]{2,1,0:T(8,128)(2,1)}, u32[]{:S(2)}) copy-start(bf16[32,8,128]{2,1,0:T(8,128)(2,1)} %get-tuple-element.17) | copy-start | bytes 196612
  11.1 7.8 %copy-start.6 = (f32[1,4]{1,0:T(1,128)S(1)}, f32[1,4]{1,0:T(1,128)}, u32[]{:S(2)}) copy-start(f32[1,4]{1,0:T(1,128)} %refs_2_.3) | copy-start | bytes 52
  13.1 2.4 %collective-permute-start.2 = (bf16[768,128]{1,0:T(8,128)(2,1)S(1)}, bf16[768,128]{1,0:T(8,128)(2,1)S(1)}, u32[]{:S(2)}, u32[]{:S(2)}) collective-permute-start(bf16[768,128]{1,0:T(8,128)(2,1)S(1)} %get-tuple-element.20.refs_1_), channel_id=1, source_target_pairs={{0,1},{1,0},{2,3},{3,2},{4,5},{5,4},{6,7},{7,6},{8,9},{9,8},{10,11... | collective-permute-start | bytes 589832 | tf_op jit(solution)/shard_map/ppermute | solution.py:380
  14.8 1.5 %collective-permute-start.5 = (bf16[768,128]{1,0:T(8,128)(2,1)S(1)}, bf16[768,128]{1,0:T(8,128)(2,1)S(1)}, u32[]{:S(2)}, u32[]{:S(2)}) collective-permute-start(bf16[768,128]{1,0:T(8,128)(2,1)S(1)} %pad_maximum_fusion), channel_id=1, source_target_pairs={{0,1},{1,0},{2,3},{3,2},{4,5},{5,4},{6,7},{7,6},{8,9},{9,8},{10,11... | collective-permute-start | bytes 589832 | tf_op jit(solution)/shard_map/ppermute | solution.py:380
  26.8 1.4 %collective-permute-start.8 = (f32[2,128,128]{2,1,0:T(8,128)S(1)}, f32[2,128,128]{2,1,0:T(8,128)S(1)}, u32[]{:S(2)}, u32[]{:S(2)}) collective-permute-start(f32[2,128,128]{2,1,0:T(8,128)S(1)} %slice.13), channel_id=1, source_target_pairs={{0,1},{1,0},{2,3},{3,2},{4,5},{5,4},{6,7},{7,6},{8,9},{9,8},{10,11... | collective-permute-start | bytes 393224 | tf_op jit(solution)/shard_map/ppermute | solution.py:380
  28.2 4.3 %collective-permute-start.9 = (f32[1,128,128]{2,1,0:T(8,128)S(1)}, f32[1,128,128]{2,1,0:T(8,128)S(1)}, u32[]{:S(2)}, u32[]{:S(2)}) collective-permute-start(f32[1,128,128]{2,1,0:T(8,128)S(1)} %slice.17), channel_id=1, source_target_pairs={{0,2},{1,3},{2,0},{3,1},{4,6},{5,7},{6,4},{7,5},{8,10},{9,11},{10,... | collective-permute-start | bytes 196616 | tf_op jit(solution)/shard_map/ppermute | solution.py:380
